TPU v7x, 128 devices: a whole 4x4x4 slice. The times are simulated.
128 devices in a mesh: col: 32 (over z, x, y_hi), row: 4 (over y_lo, core).
Axes of the slice: x: 4, y: 4 (y_hi: 2, y_lo: 2; y = y_hi * 2 + y_lo), z: 4, core: 2. Of those that a mesh axis runs over, the one named last changes fastest.
Arguments:
- inverse_block: float32 [8192, 8192], P('row', 'col'), may hold values from -6 to 6
- panels: float32 [64, 2048, 256], P('col', 'row'), may hold values from -0.125 to 0.125
- pattern: int32 [64, 8], replicated, may hold values from 0 to 31, as said below
- active: int32 [64], replicated, may hold values 0 or 1
Outputs:
- selected: float32 [16384, 8192], P('row', 'col')
Inputs may be any that keep to these rules, and one draw needn't show every extreme that they name: `pattern`: within each row, the entries g * 2 to (g + 1) * 2 - 1 are distinct and lie in g * 8 to (g + 1) * 8 - 1, for each group g of 2 consecutive entries.
All inputs are finite; a program needn't handle non-finite values.
Results may differ from a plain program's by a relative error of at most 0.0003.
Values sent between devices are 32-bit elements; how exact they have to be, the bound alone decides.
A program may use at most 256 MiB of HBM per device.

v0:
```python
import jax
import jax.numpy as jnp
from jax import lax
from jax.sharding import PartitionSpec as P


def slot_products(panel_piece, rows_used, flags, inverse_rows, offset):
    slot_count = panel_piece.shape[0]
    tile_width = panel_piece.shape[2]
    per_slot = rows_used.shape[1]
    blocks = inverse_rows.reshape(
        inverse_rows.shape[0] // tile_width, tile_width, inverse_rows.shape[1]
    )
    chosen = jnp.take(blocks, (rows_used - offset).reshape(-1), axis=0)
    chosen = chosen.reshape(slot_count, per_slot, tile_width, inverse_rows.shape[1])
    panel_tiles = panel_piece.reshape(slot_count, per_slot, tile_width, tile_width)
    product = jnp.einsum("kmab,kmac->kbc", panel_tiles, chosen, precision=lax.Precision.HIGHEST)
    factor = -flags.astype(jnp.float32)
    return (product * factor[:, None, None]).reshape(slot_count * tile_width, inverse_rows.shape[1])


def on_device(inverse_block, panels, pattern, active):
    tile_width = panels.shape[2]
    per_group = panels.shape[1] // tile_width
    row_index = lax.axis_index("row")
    rows_local = inverse_block.shape[0] // tile_width
    own_pattern = lax.dynamic_slice_in_dim(pattern, row_index * per_group, per_group, 1)
    offset = row_index * rows_local
    gathered = lax.all_gather(panels, "col", axis=0, tiled=True)
    partial_value = slot_products(gathered, own_pattern, active, inverse_block, offset)
    result = lax.psum_scatter(partial_value, "row", scatter_dimension=0, tiled=True)
    return result


def solution(mesh):
    in_specs = (P("row", "col"), P("col", "row", None), P(), P())
    out_specs = P("row", "col")
    return jax.shard_map(
        on_device, mesh=mesh, in_specs=in_specs, out_specs=out_specs, check_vma=False
    )
```

profile of v0, /device:TPU:1, one launch (start us, length us, event | category | flops | bytes accessed | tf_op | source)
XLA Modules:
  0.0 487.9 jit_solution(12037671746556430823)
XLA Ops:
  6.5 0.0 copy-start
  6.5 0.0 all-gather.2.cloned.1.call-start
  6.5 0.7 all-gather.2.cloned.1.call-update
  7.3 0.0 reduce-scatter.2.cloned.1.call-start
  7.3 0.7 compare_and_fusion
  8.0 0.1 copy.10
  8.1 0.1 copy.11
  8.2 0.1 reshape.51
  8.4 0.0 copy-done
  8.4 0.0 copy-start.1
  8.4 12.4 %gather_fusion = f32[128,256,256]{2,1,0:T(8,128)} fusion(f32[8,256,256]{2,1,0:T(8,128)S(1)} %bitcast.12, s32[1024]{0:T(1024)S(1)} %pad_clamp_fusion), kind=kCustom, calls=%fused_computation | custom fusion | bytes 67109376 | tf_op jit(solution)/shard_map/jit(_take)/gather | solution.py:14
  20.8 0.0 copy-done.1
  20.8 251.7 %all-gather.2.cloned.1.call-done = f32[64,512,256]{2,1,0:T(8,128)} async-done(((f32[2,512,256]{2,1,0:T(8,128)}), f32[64,512,256]{2,1,0:T(8,128)}) %all-gather.2.cloned.1.call-update) | async-done | bytes 33554448 | tf_op jit(solution)/shard_map/all_gather | solution.py:29
  272.5 63.6 %bitcast_multiply_fusion = f32[64,256,256]{1,2,0:T(8,128)} fusion(f32[64,2,256,256]{3,2,1,0:T(8,128)} %bitcast.15, f32[64,2,256,256]{3,2,1,0:T(8,128)} %bitcast.13, pred[64,2]{1,0:T(8,128)(4,1)S(1)} %copy.10, f32[64]{0:T(128)S(1)} %convert_negate_fusion), kind=kOutput, calls=%fused_computation.3 | convolution fusion | flops 25782386688 | bytes 83886464 | tf_op jit(solution)/shard_map/kmab,kmac->kbc/dot_general | solution.py:17
  336.0 0.0 reduce-scatter.2.cloned.1.call-update
  336.0 145.0 %reduce-scatter.2.cloned.1.call-done = f32[4096,256]{1,0:T(8,128)} async-done(((f32[16384,256]{1,0:T(8,128)}), f32[4096,256]{1,0:T(8,128)}) %reduce-scatter.2.cloned.1.call-update) | async-done | bytes 4194320 | tf_op jit(solution)/shard_map/reduce_scatter | solution.py:31
  (3 shorter events, 0.0 us)
Async XLA Ops:
  6.5 1.9 copy-start
  6.5 265.9 %all-gather.2.cloned.1.call-start = ((), (), s32[]{:S(2)}) async-start(), calls=%async_computation.1 | async-start | bytes 34603008 | tf_op jit(solution)/shard_map/all_gather | solution.py:29
  7.3 473.8 %reduce-scatter.2.cloned.1.call-start = ((), (), s32[]{:S(2)}) async-start(), calls=%async_computation.2 | async-start | bytes 20971520 | tf_op jit(solution)/shard_map/reduce_scatter | solution.py:31
  8.4 12.4 %copy-start.1 = (s32[64]{0:T(128)S(1)}, s32[64]{0:T(128)}, u32[]{:S(2)}) copy-start(s32[64]{0:T(128)} %param.7) | copy-start | bytes 772
Sparse Core Ops, SparseCore 0:
  10.4 262.0 all-gather.1
  336.2 144.8 reduce-scatter.1
where the time goes:
time: 488 us
  waiting for transfers between devices  397 us (81%)
  matrix products  63.6 us (13%)
  between operations  13.4 us (3%)
  local copies, waits for them, and re-layouts  12.7 us (3%)
    all_gather x1, waiting for transfers between devices, on_device(): gathered = lax.all_gather(panels, 'col', axis=0, tiled=True)  252 us
    reduce_scatter x1, waiting for transfers between devices, on_device(): lax.psum_scatter(partial_value, 'row', scatter_dimension=0, tiled=True)  145 us
    dot_general x1, matrix products, slot_products(): jnp.einsum('kmab,kmac->kbc', panel_tiles, chosen, precision=lax.Precision...  63.6 us
    gather x1, local copies, waits for them, and re-layouts, slot_products(): chosen = jnp.take(blocks, (rows_used - offset).reshape(-1), axis=0)  12.4 us
  transfers between devices with their start and end apart: 2, of which 2 were waited for; matrix products, arithmetic and copies ran while one was open for 3% of the time, Pallas kernels for 0%

commit v1 on v0

v1 whole, which is shorter than its diff:
```python
import functools

import jax
import jax.numpy as jnp
from jax import lax
from jax.experimental import pallas as pl
from jax.experimental.pallas import tpu as pltpu
from jax.sharding import PartitionSpec as P

MESH = pl.DeviceIdType.MESH
AXIS = 4


def split(value):
    high = value.astype(jnp.bfloat16)
    low = (value - high.astype(jnp.float32)).astype(jnp.bfloat16)
    return high, low


def kernel(
    inverse_in, panels_in, pattern, active, out,
    inverse, inv_high, inv_low, pan, give, take, mine,
    own_sem, inv_send, inv_recv, pan_send, pan_recv, core_send, core_recv, out_send, out_recv, out_local,
):
    tile = panels_in.shape[2]
    depth = panels_in.shape[1]
    rows_local = inverse_in.shape[0]

    col, row = lax.axis_index("col"), lax.axis_index("row")
    z, x, y_hi = col // (2 * AXIS), col // 2 % AXIS, col % 2
    y_lo, core = row // 2, row % 2
    y = y_hi * 2 + y_lo

    def device(x_at, y_at, z_at, core_at):
        return (z_at * 2 * AXIS + x_at * 2 + y_at // 2, y_at % 2 * 2 + core_at)

    def turn(at, by):
        return (at + by + AXIS) % AXIS

    def along(axis, by):
        if axis == "x":
            return device(turn(x, by), y, z, core)
        if axis == "y":
            return device(x, turn(y, by), z, core)
        return device(x, y, turn(z, by), core)

    partner = device(x, y_hi * 2 + 1 - y_lo, z, core)
    sibling = device(x, y, z, 1 - core)

    barrier = pltpu.get_barrier_semaphore()
    peers = [along("x", 1), along("x", -1), along("z", 1), along("z", -1)]
    peers += [along("y", 1), along("y", -1), along("y", 2), sibling]
    for peer in peers:
        pl.semaphore_signal(barrier, inc=1, device_id=peer, device_id_type=MESH)
    pl.semaphore_wait(barrier, len(peers))

    sent = []
    numbers = {"inv": 0, "pan": 0}

    def push(kind, source, target, to):
        sends, receives = (inv_send, inv_recv) if kind == "inv" else (pan_send, pan_recv)
        number = numbers[kind]
        numbers[kind] += 1
        copy = pltpu.make_async_remote_copy(
            src_ref=source, dst_ref=target, send_sem=sends.at[number], recv_sem=receives.at[number],
            device_id=to, device_id_type=MESH,
        )
        copy.start()
        sent.append(copy)
        return copy

    def home(first, by_first, by_second):
        if first == "x":
            return turn(x, by_first), turn(z, by_second)
        return turn(x, by_second), turn(z, by_first)

    def piece(at, group, half=None):
        view = pan.at[at[0], at[1], group]
        if half is not None:
            view = view.at[pl.ds(half * (depth // 2), depth // 2)]
        return view

    def spread(group, at, axis, source=None):
        target = piece(at, group)
        source = target if source is None else source
        return push("pan", source, target, along(axis, 1)), push("pan", source, target, along(axis, -1))

    def relay(group, below, above, axis, arrivals):
        arrivals[0].wait_recv()
        up = push("pan", piece(below, group, 0), piece(below, group, 0), along(axis, 1))
        arrivals[1].wait_recv()
        down = push("pan", piece(above, group, 1), piece(above, group, 1), along(axis, -1))
        return up, down

    own_home = (x, z)
    other = 1 - y_lo

    swap = push("pan", panels_in.at[other], piece(own_home, y_lo), partner)

    half_rows = rows_local // 2

    def inverse_half(at, half):
        return inverse.at[at, pl.ds(half * half_rows, half_rows)]

    def own_half(half):
        return inverse_in.at[pl.ds(half * half_rows, half_rows)]

    up_0 = push("inv", own_half(0), inverse_half(y, 0), along("y", 1))
    down_1 = push("inv", own_half(1), inverse_half(y, 1), along("y", -1))
    up_1 = push("inv", own_half(1), inverse_half(y, 1), along("y", 1))
    down_0 = push("inv", own_half(0), inverse_half(y, 0), along("y", -1))

    own_panel = panels_in.at[y_lo]
    a_first = spread(y_lo, own_home, "x", own_panel)
    a_second = {0: spread(y_lo, own_home, "z", own_panel)}

    own_inverse = pltpu.make_async_copy(inverse_in, inverse.at[y], own_sem.at[0])
    own_inverse.start()
    own_pan = pltpu.make_async_copy(own_panel, piece(own_home, y_lo), own_sem.at[1])
    own_pan.start()
    own_inverse.wait()
    own_pan.wait()

    def split_inverse(at, half):
        def body(i):
            block = half * half_rows + i
            high, low = split(inverse[at, block])
            inv_high[at, block] = high
            inv_low[at, block] = low

        pl.loop(0, half_rows)(body)

    split_inverse(y, 0)
    split_inverse(y, 1)

    a_far = relay(y_lo, home("x", -1, 0), home("x", 1, 0), "x", a_first)
    a_second[-1] = spread(y_lo, home("x", -1, 0), "z")
    a_second[1] = spread(y_lo, home("x", 1, 0), "z")
    swap.wait_recv()
    b_first = spread(other, own_home, "z")
    b_second = {0: spread(other, own_home, "x")}
    a_relays = [relay(y_lo, home("x", 0, -1), home("x", 0, 1), "z", a_second[0])]
    for copy in a_far:
        copy.wait_recv()
    a_second[2] = spread(y_lo, home("x", 2, 0), "z")
    b_far = relay(other, home("z", -1, 0), home("z", 1, 0), "z", b_first)
    b_second[-1] = spread(other, home("z", -1, 0), "x")
    b_second[1] = spread(other, home("z", 1, 0), "x")
    b_relays = [relay(other, home("z", 0, -1), home("z", 0, 1), "x", b_second[0])]

    up_0.wait_recv()
    far_0 = push("inv", inverse_half(turn(y, -1), 0), inverse_half(turn(y, -1), 0), along("y", 1))
    down_1.wait_recv()
    far_1 = push("inv", inverse_half(turn(y, 1), 1), inverse_half(turn(y, 1), 1), along("y", -1))
    split_inverse(turn(y, -1), 0)
    split_inverse(turn(y, 1), 1)

    for copy in b_far:
        copy.wait_recv()
    b_second[2] = spread(other, home("z", 2, 0), "x")
    up_1.wait_recv()
    split_inverse(turn(y, -1), 1)
    down_0.wait_recv()
    split_inverse(turn(y, 1), 0)

    for by in (-1, 1, 2):
        a_relays.append(relay(y_lo, home("x", by, -1), home("x", by, 1), "z", a_second[by]))
        b_relays.append(relay(other, home("z", by, -1), home("z", by, 1), "x", b_second[by]))

    far_0.wait_recv()
    split_inverse(turn(y, 2), 0)
    far_1.wait_recv()
    split_inverse(turn(y, 2), 1)
    for pair in a_relays + b_relays:
        for copy in pair:
            copy.wait_recv()

    def multiply(x_at, z_at, total, index):
        slot = z_at * (AXIS * AXIS) + x_at * AXIS + y
        for group in range(2):
            for entry in range(2):
                owner = group * 2 + core
                block = lax.rem(pattern[slot, owner * 2 + entry], rows_local)
                high, low = split(pan[x_at, z_at, group, pl.ds(entry * tile, tile), :].T)
                for side in range(2):
                    from_high = inv_high[side * 2 + group, block]
                    from_low = inv_low[side * 2 + group, block]
                    value = jnp.dot(high, from_high, preferred_element_type=jnp.float32)
                    value += jnp.dot(low, from_high, preferred_element_type=jnp.float32)
                    value += jnp.dot(high, from_low, preferred_element_type=jnp.float32)
                    if group == 0 and entry == 0:
                        total[index, side] = value
                    else:
                        total[index, side] += value

    def places(step):
        quarter = step % 4
        x_at = turn(x, quarter + quarter // 2 * (5 - 2 * quarter))
        z_mine = turn(z, (z + core) % 2 + step // 4 * 2)
        z_other = turn(z, (z + core + 1) % 2 + step // 4 * 2)
        return x_at, z_mine, z_other

    def across(step):
        return pltpu.make_async_remote_copy(
            src_ref=give.at[step], dst_ref=take.at[step], send_sem=core_send.at[step], recv_sem=core_recv.at[step],
            device_id=sibling, device_id_type=MESH,
        )

    def out_rows(x_at, y_at):
        return out.at[pl.ds(pl.multiple_of((x_at * AXIS + y_at) * tile, tile), tile)]

    def deliver(step, x_at, side, owner_lo, to_y):
        return pltpu.make_async_remote_copy(
            src_ref=mine.at[step, side], dst_ref=out_rows(x_at, y),
            send_sem=out_send.at[step, side], recv_sem=out_recv.at[y, x_at],
            device_id=device(x, to_y, z, core), device_id_type=MESH,
        )

    def keep(step, x_at):
        return pltpu.make_async_copy(mine.at[step, y_hi], out_rows(x_at, y), out_local.at[x_at])

    def finish(step):
        x_at, z_at, _ = places(step)
        slot = z_at * (AXIS * AXIS) + x_at * AXIS + y
        factor = -active[slot].astype(jnp.float32)
        across(step).wait_recv()
        mine[step] = (mine[step] + take[step]) * factor
        owner_lo = z_at // 2
        deliver(step, x_at, 1 - y_hi, owner_lo, (1 - y_hi) * 2 + owner_lo).start()

        @pl.when(owner_lo == y_lo)
        def _():
            keep(step, x_at).start()

        @pl.when(owner_lo != y_lo)
        def _():
            deliver(step, x_at, y_hi, owner_lo, y_hi * 2 + owner_lo).start()

    def step_body(step):
        x_at, z_mine, z_other = places(step)
        multiply(x_at, z_other, give, step)
        across(step).start()
        multiply(x_at, z_mine, mine, step)

        @pl.when(step > 0)
        def _():
            finish(step - 1)

    steps = give.shape[0]
    pl.loop(0, steps)(step_body)
    finish(steps - 1)

    def settle(step):
        x_at, z_at, _ = places(step)
        owner_lo = z_at // 2
        across(step).wait_send()
        deliver(step, x_at, 1 - y_hi, owner_lo, (1 - y_hi) * 2 + owner_lo).wait_send()

        @pl.when(owner_lo == y_lo)
        def _():
            keep(step, x_at).wait()

        @pl.when(owner_lo != y_lo)
        def _():
            deliver(step, x_at, y_hi, owner_lo, y_hi * 2 + owner_lo).wait_send()

    pl.loop(0, steps)(settle)
    for copy in sent:
        copy.wait_send()
    for by in range(1, AXIS):
        for x_at in range(AXIS):
            y_at = turn(y, by)
            pltpu.make_async_remote_copy(
                src_ref=mine.at[0, 0], dst_ref=out_rows(x_at, y_at),
                send_sem=out_send.at[0, 0], recv_sem=out_recv.at[y_at, x_at],
                device_id=along("y", by), device_id_type=MESH,
            ).wait_recv()


def on_device(inverse_block, panels, pattern, active):
    rows, tile = inverse_block.shape
    rows_local = rows // tile
    depth = panels.shape[1]
    steps = AXIS * AXIS // 2
    dma = pltpu.SemaphoreType.DMA
    return pl.pallas_call(
        kernel,
        out_shape=jax.ShapeDtypeStruct((AXIS * AXIS * tile, tile), jnp.float32),
        in_specs=[pl.BlockSpec(memory_space=pl.ANY)] * 2 + [pl.BlockSpec(memory_space=pltpu.SMEM)] * 2,
        out_specs=pl.BlockSpec(memory_space=pl.ANY),
        scratch_shapes=[
            pltpu.VMEM((AXIS, rows_local, tile, tile), jnp.float32),
            pltpu.VMEM((AXIS, rows_local, tile, tile), jnp.bfloat16),
            pltpu.VMEM((AXIS, rows_local, tile, tile), jnp.bfloat16),
            pltpu.VMEM((AXIS, AXIS, 2, depth, tile), jnp.float32),
            pltpu.VMEM((steps, 2, tile, tile), jnp.float32),
            pltpu.VMEM((steps, 2, tile, tile), jnp.float32),
            pltpu.VMEM((steps, 2, tile, tile), jnp.float32),
            dma((2,)),
            dma((6,)), dma((6,)),
            dma((41,)), dma((41,)),
            dma((steps,)), dma((steps,)),
            dma((steps, 2)), dma((AXIS, AXIS)), dma((AXIS,)),
        ],
        compiler_params=pltpu.CompilerParams(
            collective_id=0, has_side_effects=True, vmem_limit_bytes=56 * 1024 * 1024
        ),
        cost_estimate=pl.CostEstimate(flops=6 * 128 * tile**3, bytes_accessed=20 * 1024 * 1024, transcendentals=0),
        name="selected_inverse",
    )(inverse_block.reshape(rows_local, tile, tile), panels, pattern, active)


def solution(mesh):
    in_specs = (P("row", "col"), P("col", "row", None), P(), P())
    out_specs = P("row", "col")
    return jax.shard_map(
        on_device, mesh=mesh, in_specs=in_specs, out_specs=out_specs, check_vma=False
    )
```

time: 488 us -> 179 us (0.37)
  waiting for transfers between devices: 397 us -> 0 us
  Pallas kernels: 0 us -> 170 us
  matrix products: 63.6 us -> 0 us
  between operations: 13.4 us -> 0.01 us
  local copies, waits for them, and re-layouts: 12.7 us -> 5.85 us
    all_gather x1 -> x0, waiting for transfers between devices: 252 us -> none  [on_device(): gathered = lax.all_gather(panels, 'col', axis=0, tiled=True)]
    pallas_call x0 -> x1, Pallas kernels: none -> 170 us  [on_device(): pl.pallas_call(kernel, out_shape=jax.ShapeDtypeStruct((AXIS * AXIS * tile...]
    reduce_scatter x1 -> x0, waiting for transfers between devices: 145 us -> none  [on_device(): lax.psum_scatter(partial_value, 'row', scatter_dimension=0, tiled=True)]
    dot_general x1 -> x0, matrix products: 63.6 us -> none  [slot_products(): jnp.einsum('kmab,kmac->kbc', panel_tiles, chosen, precision=lax.Precision...]
    gather x1 -> x0, local copies, waits for them, and re-layouts: 12.4 us -> none  [slot_products(): chosen = jnp.take(blocks, (rows_used - offset).reshape(-1), axis=0)]
    unnamed x4 -> x2, local copies, waits for them, and re-layouts: 0.01 us -> 5.85 us
  transfers between devices with their start and end apart: 2 -> 0, of which waited for: 2 -> 0; matrix products, arithmetic and copies ran while one was open for 3% -> 0% of each run, Pallas kernels for 0% -> 0%
where the time goes in v1:
time: 179 us; the launch traced here: 176 us
  Pallas kernels  170 us (95%)
  local copies, waits for them, and re-layouts  5.85 us (3%)
    pallas_call x1, Pallas kernels, on_device(): pl.pallas_call(kernel, out_shape=jax.ShapeDtypeStruct((AXIS * AXIS * tile...  170 us
    unnamed x2, local copies, waits for them, and re-layouts  5.85 us

profile of v1, /device:TPU:1, one launch (start us, length us, event | category | flops | bytes accessed | tf_op | source)
XLA Modules:
  0.0 176.3 jit_solution(18436904605267090542)
XLA Ops:
  0.0 1.4 copy.5.pattern
  1.4 170.4 %selected_inverse.1 = f32[4096,256]{1,0:T(8,128)} custom-call(f32[8,256,256]{2,1,0:T(8,128)} %bitcast.1, f32[2,512,256]{2,1,0:T(8,128)} %panels_in.1, s32[64,8]{1,0:T(8,128)} %copy.5.pattern, s32[64]{0:T(128)} %active.1), custom_call_target="tpu_custom_call" | custom-call | flops 12884901888 | bytes 20971520 | tf_op jit(solution)/shard_map/selected_inverse/pallas_call | solution.py:286
  171.8 4.5 %copy.7 = f32[4096,256]{1,0:T(8,128)} copy(f32[4096,256]{1,0:T(8,128)} %selected_inverse.1) | data formatting | bytes 8388608

commit v2 on v1

v2 whole, which is shorter than its diff:
```python
import functools

import jax
import jax.numpy as jnp
from jax import lax
from jax.experimental import pallas as pl
from jax.experimental.pallas import tpu as pltpu
from jax.sharding import PartitionSpec as P

MESH = pl.DeviceIdType.MESH
AXIS = 4


def split(value):
    high = value.astype(jnp.bfloat16)
    low = (value - high.astype(jnp.float32)).astype(jnp.bfloat16)
    return high, low


def kernel(
    inverse_in, panels_in, pattern, active, out,
    inverse, inv_high, inv_low, pan, give, take, mine,
    own_sem, inv_send, inv_recv, pan_send, pan_recv, core_send, core_recv, out_send, out_recv, out_local,
):
    tile = panels_in.shape[3]
    rows_local = inverse_in.shape[0]

    col, row = lax.axis_index("col"), lax.axis_index("row")
    z, x, y_hi = col // (2 * AXIS), col // 2 % AXIS, col % 2
    y_lo, core = row // 2, row % 2
    y = y_hi * 2 + y_lo

    def device(x_at, y_at, z_at, core_at):
        return (z_at * 2 * AXIS + x_at * 2 + y_at // 2, y_at % 2 * 2 + core_at)

    def turn(at, by):
        return (at + by + AXIS) % AXIS

    def along(axis, by):
        if axis == "x":
            return device(turn(x, by), y, z, core)
        if axis == "y":
            return device(x, turn(y, by), z, core)
        return device(x, y, turn(z, by), core)

    partner = device(x, y_hi * 2 + 1 - y_lo, z, core)
    sibling = device(x, y, z, 1 - core)

    barrier = pltpu.get_barrier_semaphore()
    peers = [along("x", 1), along("x", -1), along("z", 1), along("z", -1)]
    peers += [along("y", 1), along("y", -1), along("y", 2), sibling]
    for peer in peers:
        pl.semaphore_signal(barrier, inc=1, device_id=peer, device_id_type=MESH)
    pl.semaphore_wait(barrier, len(peers))

    sent = []

    def push(kind, source, target, to):
        sends, receives = (inv_send, inv_recv) if kind == "inv" else (pan_send, pan_recv)
        number = len([held for held in sent if held[0] == kind])
        copy = pltpu.make_async_remote_copy(
            src_ref=source, dst_ref=target, send_sem=sends.at[number], recv_sem=receives.at[number],
            device_id=to, device_id_type=MESH,
        )
        copy.start()
        sent.append((kind, copy))
        return copy

    class Way:
        def __init__(self, group, entry, first, second):
            self.group, self.entry, self.first, self.second = group, entry, first, second
            self.flying = {}

        def view(self, by_first, by_second, half=None):
            by_x, by_z = (by_first, by_second) if self.first == "x" else (by_second, by_first)
            tile_at = pan.at[turn(x, by_x), turn(z, by_z), self.group, self.entry]
            return tile_at if half is None else tile_at.at[pl.ds(half * (tile // 2), tile // 2)]

        def spread(self, key, axis, at, source=None):
            source = self.view(*at) if source is None else source
            self.flying[key] = [push("pan", source, self.view(*at), along(axis, by)) for by in (1, -1)]

        def relay(self, key, axis, at_below, at_above):
            up, down = self.flying[key]
            up.wait_recv()
            below = self.view(*at_below, half=0)
            far_up = push("pan", below, below, along(axis, 1))
            down.wait_recv()
            above = self.view(*at_above, half=1)
            far_down = push("pan", above, above, along(axis, -1))
            self.flying[key] = [far_up, far_down]

        def settle(self, key):
            for copy in self.flying.pop(key):
                copy.wait_recv()

        def start(self, source=None):
            self.spread("first", self.first, (0, 0), source)

        def pass_on(self):
            self.relay("first", self.first, (-1, 0), (1, 0))

        def passed(self):
            self.settle("first")

        def turn_off(self, by, source=None):
            self.spread(by, self.second, (by, 0), source)

        def turned_on(self, by):
            self.relay(by, self.second, (by, -1), (by, 1))

        def arrived(self, by):
            self.settle(by)

    other = 1 - y_lo
    near = [Way(y_lo, 0, "x", "z"), Way(y_lo, 1, "z", "x")]
    pair = [Way(other, 0, "x", "z"), Way(other, 1, "z", "x")]
    both = near + pair

    swap = push("pan", panels_in.at[other], pan.at[x, z, y_lo], partner)

    half_rows = rows_local // 2

    def inverse_half(at, half):
        return inverse.at[at, pl.ds(half * half_rows, half_rows)]

    def own_half(half):
        return inverse_in.at[pl.ds(half * half_rows, half_rows)]

    up_0 = push("inv", own_half(0), inverse_half(y, 0), along("y", 1))
    down_1 = push("inv", own_half(1), inverse_half(y, 1), along("y", -1))
    up_1 = push("inv", own_half(1), inverse_half(y, 1), along("y", 1))
    down_0 = push("inv", own_half(0), inverse_half(y, 0), along("y", -1))

    for entry, way in enumerate(near):
        way.start(panels_in.at[y_lo, entry])
    for entry, way in enumerate(near):
        way.turn_off(0, panels_in.at[y_lo, entry])

    own_inverse = pltpu.make_async_copy(inverse_in, inverse.at[y], own_sem.at[0])
    own_inverse.start()
    own_pan = pltpu.make_async_copy(panels_in.at[y_lo], pan.at[x, z, y_lo], own_sem.at[1])
    own_pan.start()
    own_inverse.wait()
    own_pan.wait()

    def split_inverse(at, half):
        def body(i):
            block = half * half_rows + i
            high, low = split(inverse[at, block])
            inv_high[at, block] = high
            inv_low[at, block] = low

        pl.loop(0, half_rows)(body)

    def multiply(x_at, z_at, total, step, side):
        slot = z_at * (AXIS * AXIS) + x_at * AXIS + y
        column = (y_hi + side) % 2
        for group in range(2):
            for entry in range(2):
                block = lax.rem(pattern[(group * 2 + core) * 2 + entry, slot], rows_local)
                high, low = split(pan[x_at, z_at, group, entry].T)
                from_high = inv_high[column * 2 + group, block]
                from_low = inv_low[column * 2 + group, block]
                value = jnp.dot(high, from_high, preferred_element_type=jnp.float32)
                value += jnp.dot(low, from_high, preferred_element_type=jnp.float32)
                value += jnp.dot(high, from_low, preferred_element_type=jnp.float32)
                if group == 0 and entry == 0:
                    total[step, side] = value
                else:
                    total[step, side] += value

    def places(step):
        quarter = step // 2
        x_at = turn(x, quarter + quarter // 2 * (5 - 2 * quarter))
        return x_at, (y_lo + 1 + step % 2) % 2

    def across(step, side):
        return pltpu.make_async_remote_copy(
            src_ref=give.at[step, side], dst_ref=take.at[step, side],
            send_sem=core_send.at[step, side], recv_sem=core_recv.at[step, side],
            device_id=sibling, device_id_type=MESH,
        )

    def out_rows(x_at, y_at):
        return out.at[pl.ds(pl.multiple_of((x_at * AXIS + y_at) * tile, tile), tile)]

    def deliver(step, side, x_at, to_y):
        return pltpu.make_async_remote_copy(
            src_ref=mine.at[step, side], dst_ref=out_rows(x_at, y),
            send_sem=out_send.at[step, side], recv_sem=out_recv.at[y, x_at],
            device_id=device(x, to_y, z, core), device_id_type=MESH,
        )

    def keep(step, side, x_at):
        return pltpu.make_async_copy(mine.at[step, side], out_rows(x_at, y), out_local.at[x_at])

    def finish(step, side):
        x_at, owner_lo = places(step)
        slot = (owner_lo * 2 + core) * (AXIS * AXIS) + x_at * AXIS + y
        factor = -active[slot].astype(jnp.float32)
        across(step, side).wait_recv()
        mine[step, side] = (mine[step, side] + take[step, side]) * factor
        to_y = (y_hi + side) % 2 * 2 + owner_lo

        @pl.when(to_y == y)
        def _():
            keep(step, side, x_at).start()

        @pl.when(to_y != y)
        def _():
            deliver(step, side, x_at, to_y).start()

    last = []

    def units(first, count, side):
        before = last[-1] if last else None

        def body(i):
            step = first + i
            x_at, owner_lo = places(step)
            multiply(x_at, owner_lo * 2 + 1 - core, give, step, side)
            across(step, side).start()
            multiply(x_at, owner_lo * 2 + core, mine, step, side)
            if before is None:

                @pl.when(i > 0)
                def _():
                    finish(step - 1, side)

            else:
                finish(jnp.where(i > 0, step - 1, before[0]), jnp.where(i > 0, side, before[1]))

        pl.loop(0, count)(body)
        last.append((first + count - 1, side))

    split_inverse(y, 0)
    split_inverse(y, 1)
    for way in near:
        way.pass_on()
    for way in near:
        way.turn_off(-1)
    swap.wait_recv()
    for way in pair:
        way.start()
    for way in near:
        way.turned_on(0)
    for way in pair:
        way.turn_off(0)
    for way in near:
        way.turn_off(1)
    for way in near:
        way.passed()
        way.turn_off(2)
    for way in pair:
        way.pass_on()
    for way in pair:
        way.turned_on(0)
    for way in near:
        way.turned_on(-1)
    for way in pair:
        way.turn_off(1)
        way.turn_off(-1)
    for way in pair:
        way.passed()
        way.turn_off(2)
    up_0.wait_recv()
    far_0 = push("inv", inverse_half(turn(y, -1), 0), inverse_half(turn(y, -1), 0), along("y", 1))
    down_1.wait_recv()
    far_1 = push("inv", inverse_half(turn(y, 1), 1), inverse_half(turn(y, 1), 1), along("y", -1))
    split_inverse(turn(y, -1), 0)
    split_inverse(turn(y, 1), 1)
    for by in (1, 2):
        for way in near:
            way.turned_on(by)
    for by in (1, -1):
        for way in pair:
            way.turned_on(by)
    up_1.wait_recv()
    split_inverse(turn(y, -1), 1)
    down_0.wait_recv()
    split_inverse(turn(y, 1), 0)
    for way in both:
        way.arrived(0)
    units(0, 2, 0)
    for way in pair:
        way.turned_on(2)
    for way in near:
        for by in (1, -1, 2):
            way.arrived(by)
    for way in pair:
        way.arrived(1)
    units(2, 2, 0)
    far_0.wait_recv()
    split_inverse(turn(y, 2), 0)
    far_1.wait_recv()
    split_inverse(turn(y, 2), 1)
    units(0, 4, 1)
    for way in pair:
        way.arrived(-1)
    units(4, 2, 0)
    units(4, 2, 1)
    for way in pair:
        way.arrived(2)
    units(6, 2, 0)
    units(6, 2, 1)
    finish(*last[-1])

    steps = give.shape[0]

    def settle(number):
        step, side = number // 2, number % 2
        x_at, owner_lo = places(step)
        to_y = (y_hi + side) % 2 * 2 + owner_lo
        across(step, side).wait_send()

        @pl.when(to_y == y)
        def _():
            keep(step, side, x_at).wait()

        @pl.when(to_y != y)
        def _():
            deliver(step, side, x_at, to_y).wait_send()

    pl.loop(0, steps * 2)(settle)
    for _, copy in sent:
        copy.wait_send()
    for by in range(1, AXIS):
        for x_at in range(AXIS):
            y_at = turn(y, by)
            pltpu.make_async_remote_copy(
                src_ref=mine.at[0, 0], dst_ref=out_rows(x_at, y_at),
                send_sem=out_send.at[0, 0], recv_sem=out_recv.at[y_at, x_at],
                device_id=along("y", by), device_id_type=MESH,
            ).wait_recv()


def on_device(inverse_block, panels, pattern, active):
    rows, tile = inverse_block.shape
    rows_local = rows // tile
    per_group = panels.shape[1] // tile
    steps = AXIS * AXIS // 2
    dma = pltpu.SemaphoreType.DMA
    return pl.pallas_call(
        kernel,
        out_shape=jax.ShapeDtypeStruct((AXIS * AXIS * tile, tile), jnp.float32),
        in_specs=[pl.BlockSpec(memory_space=pl.ANY)] * 2 + [pl.BlockSpec(memory_space=pltpu.SMEM)] * 2,
        out_specs=pl.BlockSpec(memory_space=pl.ANY),
        scratch_shapes=[
            pltpu.VMEM((AXIS, rows_local, tile, tile), jnp.float32),
            pltpu.VMEM((AXIS, rows_local, tile, tile), jnp.bfloat16),
            pltpu.VMEM((AXIS, rows_local, tile, tile), jnp.bfloat16),
            pltpu.VMEM((AXIS, AXIS, 2, per_group, tile, tile), jnp.float32),
            pltpu.VMEM((steps, 2, tile, tile), jnp.float32),
            pltpu.VMEM((steps, 2, tile, tile), jnp.float32),
            pltpu.VMEM((steps, 2, tile, tile), jnp.float32),
            dma((2,)),
            dma((6,)), dma((6,)),
            dma((81,)), dma((81,)),
            dma((steps, 2)), dma((steps, 2)),
            dma((steps, 2)), dma((AXIS, AXIS)), dma((AXIS,)),
        ],
        compiler_params=pltpu.CompilerParams(
            collective_id=0, has_side_effects=True, vmem_limit_bytes=56 * 1024 * 1024
        ),
        cost_estimate=pl.CostEstimate(flops=6 * 128 * tile**3, bytes_accessed=20 * 1024 * 1024, transcendentals=0),
        name="selected_inverse",
    )(
        inverse_block.reshape(rows_local, tile, tile),
        panels.reshape(panels.shape[0], per_group, tile, tile),
        pattern.T,
        active,
    )


def solution(mesh):
    in_specs = (P("row", "col"), P("col", "row", None), P(), P())
    out_specs = P("row", "col")
    return jax.shard_map(
        on_device, mesh=mesh, in_specs=in_specs, out_specs=out_specs, check_vma=False
    )
```

time: 179 us -> 151 us (0.84)
  Pallas kernels: 170 us -> 145 us
    pallas_call x1, Pallas kernels: 170 us -> 145 us  [on_device(): pl.pallas_call(kernel, out_shape=jax.ShapeDtypeStruct((AXIS * AXIS * tile...]
    unnamed x2 -> x1, local copies, waits for them, and re-layouts: 5.85 us -> 4.47 us
where the time goes in v2:
time: 151 us; the launch traced here: 149 us
  Pallas kernels  145 us (96%)
  local copies, waits for them, and re-layouts  4.47 us (3%)
    pallas_call x1, Pallas kernels, on_device(): pl.pallas_call(kernel, out_shape=jax.ShapeDtypeStruct((AXIS * AXIS * tile...  145 us
    unnamed x1, local copies, waits for them, and re-layouts  4.47 us

profile of v2, /device:TPU:1, one launch (start us, length us, event | category | flops | bytes accessed | tf_op | source)
XLA Modules:
  0.0 149.5 jit_solution(13409173681629546634)
XLA Ops:
  0.0 145.0 %selected_inverse.1 = f32[4096,256]{1,0:T(8,128)} custom-call(f32[8,256,256]{2,1,0:T(8,128)} %bitcast.3, f32[2,2,256,256]{3,2,1,0:T(8,128)} %bitcast.4, s32[8,64]{1,0:T(8,128)} %bitcast.5, s32[64]{0:T(128)} %active.1), custom_call_target="tpu_custom_call" | custom-call | flops 12884901888 | bytes 20971520 | tf_op jit(solution)/shard_map/selected_inverse/pallas_call | solution.py:344
  145.0 4.5 %copy.6 = f32[4096,256]{1,0:T(8,128)} copy(f32[4096,256]{1,0:T(8,128)} %selected_inverse.1) | data formatting | bytes 8388608

commit v3 on v2

v3 whole, which is shorter than its diff:
```python
import functools

import jax
import jax.numpy as jnp
from jax import lax
from jax.experimental import pallas as pl
from jax.experimental.pallas import tpu as pltpu
from jax.sharding import PartitionSpec as P

MESH = pl.DeviceIdType.MESH
AXIS = 4


def split(value):
    high = value.astype(jnp.bfloat16)
    low = (value - high.astype(jnp.float32)).astype(jnp.bfloat16)
    return high, low


def kernel(
    inverse_in, panels_in, pattern, active, out,
    inverse, inv_high, inv_low, pan, give, take, mine,
    own_sem, inv_send, inv_recv, pan_send, pan_recv, core_send, core_recv, out_send, out_recv, out_local,
):
    tile = panels_in.shape[3]
    rows_local = inverse_in.shape[0]

    col, row = lax.axis_index("col"), lax.axis_index("row")
    z, x, y_hi = col // (2 * AXIS), col // 2 % AXIS, col % 2
    y_lo, core = row // 2, row % 2
    y = y_hi * 2 + y_lo

    def device(x_at, y_at, z_at, core_at):
        return (z_at * 2 * AXIS + x_at * 2 + y_at // 2, y_at % 2 * 2 + core_at)

    def turn(at, by):
        return (at + by + AXIS) % AXIS

    def along(axis, by):
        if axis == "x":
            return device(turn(x, by), y, z, core)
        if axis == "y":
            return device(x, turn(y, by), z, core)
        return device(x, y, turn(z, by), core)

    y_pair, y_outer, y_far = y_hi * 2 + 1 - y_lo, (1 - y_hi) * 2 + 1 - y_lo, (1 - y_hi) * 2 + y_lo
    to_pair, to_outer, to_far = (device(x, y_at, z, core) for y_at in (y_pair, y_outer, y_far))
    sibling = device(x, y, z, 1 - core)

    barrier = pltpu.get_barrier_semaphore()
    peers = [along("x", 1), along("x", -1), along("z", 1), along("z", -1)]
    peers += [to_pair, to_outer, to_far, sibling]
    for peer in peers:
        pl.semaphore_signal(barrier, inc=1, device_id=peer, device_id_type=MESH)
    pl.semaphore_wait(barrier, len(peers))

    sent = []

    def push(kind, source, target, to):
        sends, receives = (inv_send, inv_recv) if kind == "inv" else (pan_send, pan_recv)
        number = len([entry for entry in sent if entry[0] == kind])
        copy = pltpu.make_async_remote_copy(
            src_ref=source, dst_ref=target, send_sem=sends.at[number], recv_sem=receives.at[number],
            device_id=to, device_id_type=MESH,
        )
        copy.start()
        sent.append((kind, copy))
        return copy

    class Way:
        def __init__(self, group, entry, first, second):
            self.group, self.entry, self.first, self.second = group, entry, first, second
            self.flying = {}

        def view(self, by_first, by_second, half=None):
            by_x, by_z = (by_first, by_second) if self.first == "x" else (by_second, by_first)
            tile_at = pan.at[turn(x, by_x), turn(z, by_z), self.group, self.entry]
            return tile_at if half is None else tile_at.at[pl.ds(half * (tile // 2), tile // 2)]

        def spread(self, key, axis, at, source=None):
            source = self.view(*at) if source is None else source
            self.flying[key] = [push("pan", source, self.view(*at), along(axis, by)) for by in (1, -1)]

        def relay(self, key, axis, at_below, at_above):
            up, down = self.flying[key]
            up.wait_recv()
            below = self.view(*at_below, half=0)
            far_up = push("pan", below, below, along(axis, 1))
            down.wait_recv()
            above = self.view(*at_above, half=1)
            far_down = push("pan", above, above, along(axis, -1))
            self.flying[key] = [far_up, far_down]

        def settle(self, key):
            for copy in self.flying.pop(key):
                copy.wait_recv()

        def start(self, source=None):
            self.spread("first", self.first, (0, 0), source)

        def pass_on(self):
            self.relay("first", self.first, (-1, 0), (1, 0))

        def passed(self):
            self.settle("first")

        def turn_off(self, by, source=None):
            self.spread(by, self.second, (by, 0), source)

        def turned_on(self, by):
            self.relay(by, self.second, (by, -1), (by, 1))

        def arrived(self, by):
            self.settle(by)

    other = 1 - y_lo
    near = [Way(y_lo, 0, "x", "z"), Way(y_lo, 1, "z", "x")]
    pair = [Way(other, 0, "x", "z"), Way(other, 1, "z", "x")]
    both = near + pair

    swap = push("pan", panels_in.at[other], pan.at[x, z, y_lo], to_pair)

    lanes = tile // 2
    cut = rows_local * 5 // 8
    spans = (pl.ds(0, cut), pl.ds(cut, rows_local - cut))

    def columns(part):
        return slice(None) if part is None else slice(part * lanes, (part + 1) * lanes)

    def own(part, span):
        return inverse_in.at[spans[span], :, pl.ds(part * lanes, lanes)]

    def held(part, y_at, span):
        return inverse.at[part, y_at, spans[span]]

    def give_own(part, span, to):
        return push("inv", own(part, span), held(part, y, span), to)

    def relay_inverse(part, span, y_at, to):
        return push("inv", held(part, y_at, span), held(part, y_at, span), to)

    pair_0, outer_0, pair_1, outer_1, far_0, far_1 = ([None, None] for _ in range(6))
    pair_0[0] = give_own(0, 0, to_pair)
    outer_0[0] = give_own(0, 1, to_outer)
    pair_1[0] = give_own(0, 1, to_pair)
    outer_1[0] = give_own(0, 0, to_outer)

    for entry, way in enumerate(near):
        way.start(panels_in.at[y_lo, entry])
    for entry, way in enumerate(near):
        way.turn_off(0, panels_in.at[y_lo, entry])

    own_copies = [
        pltpu.make_async_copy(inverse_in.at[:, :, pl.ds(part * lanes, lanes)], inverse.at[part, y], own_sem.at[part])
        for part in range(2)
    ]
    own_copies.append(pltpu.make_async_copy(panels_in.at[y_lo], pan.at[x, z, y_lo], own_sem.at[2]))
    for copy in own_copies:
        copy.start()
    for copy in own_copies:
        copy.wait()

    def split_inverse(part, y_at, first=0, last=rows_local):
        def body(block):
            high, low = split(inverse[part, y_at, block])
            inv_high[y_at, block, :, columns(part)] = high
            inv_low[y_at, block, :, columns(part)] = low

        pl.loop(first, last)(body)

    def multiply(x_at, z_at, total, step, side, part):
        slot = z_at * (AXIS * AXIS) + x_at * AXIS + y
        column = (y_hi + side) % 2
        at = (step, side, slice(None), columns(part))
        for group in range(2):
            for entry in range(2):
                block = lax.rem(pattern[(group * 2 + core) * 2 + entry, slot], rows_local)
                high, low = split(pan[x_at, z_at, group, entry].T)
                from_high = inv_high[column * 2 + group, block, :, columns(part)]
                from_low = inv_low[column * 2 + group, block, :, columns(part)]
                value = jnp.dot(high, from_high, preferred_element_type=jnp.float32)
                value += jnp.dot(low, from_high, preferred_element_type=jnp.float32)
                value += jnp.dot(high, from_low, preferred_element_type=jnp.float32)
                if group == 0 and entry == 0:
                    total[at] = value
                else:
                    total[at] += value

    def places(step):
        quarter = step // 2
        x_at = turn(x, quarter + quarter // 2 * (5 - 2 * quarter))
        return x_at, (y_lo + 1 + step % 2) % 2

    def cell(ref, step, side, part):
        if part is None:
            return ref.at[step, side]
        return ref.at[step, side, :, pl.ds(part * lanes, lanes)]

    def across(step, side, part):
        return pltpu.make_async_remote_copy(
            src_ref=cell(give, step, side, part), dst_ref=cell(take, step, side, part),
            send_sem=core_send.at[step, side, part or 0], recv_sem=core_recv.at[step, side, part or 0],
            device_id=sibling, device_id_type=MESH,
        )

    def out_rows(x_at, y_at, part):
        rows = out.at[pl.ds(pl.multiple_of((x_at * AXIS + y_at) * tile, tile), tile)]
        return rows if part is None else rows.at[:, pl.ds(part * lanes, lanes)]

    def deliver(step, side, part, x_at, to_y):
        return pltpu.make_async_remote_copy(
            src_ref=cell(mine, step, side, part), dst_ref=out_rows(x_at, y, part),
            send_sem=out_send.at[step, side, part or 0], recv_sem=out_recv.at[y, x_at, part or 0],
            device_id=device(x, to_y, z, core), device_id_type=MESH,
        )

    def keep(step, side, part, x_at):
        return pltpu.make_async_copy(
            cell(mine, step, side, part), out_rows(x_at, y, part), out_local.at[x_at, part or 0]
        )

    def finish(step, side, part):
        x_at, owner_lo = places(step)
        slot = (owner_lo * 2 + core) * (AXIS * AXIS) + x_at * AXIS + y
        factor = -active[slot].astype(jnp.float32)
        across(step, side, part).wait_recv()
        at = (step, side, slice(None), columns(part))
        mine[at] = (mine[at] + take[at]) * factor
        to_y = (y_hi + side) % 2 * 2 + owner_lo

        @pl.when(to_y == y)
        def _():
            keep(step, side, part, x_at).start()

        @pl.when(to_y != y)
        def _():
            deliver(step, side, part, x_at, to_y).start()

    done = []

    def units(first, count, side, part=None):
        before = done[-1] if done else None

        def body(i):
            step = first + i
            x_at, owner_lo = places(step)
            multiply(x_at, owner_lo * 2 + 1 - core, give, step, side, part)
            across(step, side, part).start()
            if before is not None:

                @pl.when(i == 0)
                def _():
                    finish(*before)

            @pl.when(i > 0)
            def _():
                finish(step - 1, side, part)

            multiply(x_at, owner_lo * 2 + core, mine, step, side, part)

        pl.loop(0, count)(body)
        done.append((first + count - 1, side, part))

    def relays(ways, *places_along):
        for by in places_along:
            for way in ways:
                way.turned_on(by)

    def turns(ways, *places_along):
        for by in places_along:
            for way in ways:
                way.turn_off(by)

    def arrivals(ways, *places_along):
        for by in places_along:
            for way in ways:
                way.arrived(by)

    split_inverse(0, y)
    split_inverse(1, y)
    for way in near:
        way.pass_on()
    turns(near, -1)
    outer_0[0].wait_recv()
    far_1[0] = relay_inverse(0, 1, y_outer, to_pair)
    outer_0[1] = give_own(1, 1, to_outer)
    swap.wait_recv()
    for way in pair:
        way.start()
    relays(near, 0)
    turns(pair, 0)
    turns(near, 1)
    for way in near:
        way.passed()
    turns(near, 2)
    pair_0[0].wait_recv()
    far_0[0] = relay_inverse(0, 0, y_pair, to_outer)
    pair_0[1] = give_own(1, 0, to_pair)
    pair_1[1] = give_own(1, 1, to_pair)
    outer_1[1] = give_own(1, 0, to_outer)
    split_inverse(0, y_pair, 0, cut)
    split_inverse(0, y_outer, cut, rows_local)
    for way in pair:
        way.pass_on()
    relays(pair, 0)
    relays(near, -1)
    turns(pair, 1, -1)
    pair_1[0].wait_recv()
    outer_1[0].wait_recv()
    split_inverse(0, y_pair, cut, rows_local)
    split_inverse(0, y_outer, 0, cut)
    outer_0[1].wait_recv()
    far_1[1] = relay_inverse(1, 1, y_outer, to_pair)
    for way in pair:
        way.passed()
    turns(pair, 2)
    relays(near, 1)
    far_1[0].wait_recv()
    far_0[0].wait_recv()
    split_inverse(0, y_far)
    pair_0[1].wait_recv()
    far_0[1] = relay_inverse(1, 0, y_pair, to_outer)
    split_inverse(1, y_pair, 0, cut)
    split_inverse(1, y_outer, cut, rows_local)
    relays(near, 2)
    relays(pair, 1)
    arrivals(both, 0)
    units(0, 2, 1, 0)
    units(0, 2, 0, 0)
    relays(pair, -1)
    pair_1[1].wait_recv()
    outer_1[1].wait_recv()
    split_inverse(1, y_pair, cut, rows_local)
    split_inverse(1, y_outer, 0, cut)
    relays(pair, 2)
    far_0[1].wait_recv()
    far_1[1].wait_recv()
    split_inverse(1, y_far)
    units(0, 2, 1, 1)
    units(0, 2, 0, 1)
    arrivals(near, 1, -1, 2)
    arrivals(pair, 1)
    units(2, 2, 1)
    units(2, 2, 0)
    arrivals(pair, -1)
    units(4, 2, 1)
    units(4, 2, 0)
    arrivals(pair, 2)
    units(6, 2, 1)
    units(6, 2, 0)
    finish(*done[-1])

    steps = give.shape[0]

    def settle(number, parts):
        step, side = number // 2, number % 2
        x_at, owner_lo = places(step)
        to_y = (y_hi + side) % 2 * 2 + owner_lo
        for part in parts:
            across(step, side, part).wait_send()

        @pl.when(to_y == y)
        def _():
            for part in parts:
                keep(step, side, part, x_at).wait()

        @pl.when(to_y != y)
        def _():
            for part in parts:
                deliver(step, side, part, x_at, to_y).wait_send()

    pl.loop(0, 4)(functools.partial(settle, parts=(0, 1)))
    pl.loop(4, steps * 2)(functools.partial(settle, parts=(None,)))
    for _, copy in sent:
        copy.wait_send()
    for y_at in (y_pair, y_outer, y_far):
        for by in range(AXIS):
            x_at = turn(x, by)
            for part in (0, 1) if by == 0 else (None,):
                pltpu.make_async_remote_copy(
                    src_ref=cell(mine, 0, 0, part), dst_ref=out_rows(x_at, y_at, part),
                    send_sem=out_send.at[0, 0, 0], recv_sem=out_recv.at[y_at, x_at, part or 0],
                    device_id=to_pair, device_id_type=MESH,
                ).wait_recv()


def on_device(inverse_block, panels, pattern, active):
    rows, tile = inverse_block.shape
    rows_local = rows // tile
    per_group = panels.shape[1] // tile
    steps = AXIS * AXIS // 2
    dma = pltpu.SemaphoreType.DMA
    return pl.pallas_call(
        kernel,
        out_shape=pltpu.VMEM((AXIS * AXIS * tile, tile), jnp.float32),
        in_specs=[pl.BlockSpec(memory_space=pl.ANY)] * 2 + [pl.BlockSpec(memory_space=pltpu.SMEM)] * 2,
        out_specs=pl.BlockSpec(memory_space=pltpu.VMEM),
        scratch_shapes=[
            pltpu.VMEM((2, AXIS, rows_local, tile, tile // 2), jnp.float32),
            pltpu.VMEM((AXIS, rows_local, tile, tile), jnp.bfloat16),
            pltpu.VMEM((AXIS, rows_local, tile, tile), jnp.bfloat16),
            pltpu.VMEM((AXIS, AXIS, 2, per_group, tile, tile), jnp.float32),
            pltpu.VMEM((steps, 2, tile, tile), jnp.float32),
            pltpu.VMEM((steps, 2, tile, tile), jnp.float32),
            pltpu.VMEM((steps, 2, tile, tile), jnp.float32),
            dma((3,)),
            dma((12,)), dma((12,)),
            dma((81,)), dma((81,)),
            dma((steps, 2, 2)), dma((steps, 2, 2)),
            dma((steps, 2, 2)), dma((AXIS, AXIS, 2)), dma((AXIS, 2)),
        ],
        compiler_params=pltpu.CompilerParams(
            collective_id=0, has_side_effects=True, vmem_limit_bytes=56 * 1024 * 1024
        ),
        cost_estimate=pl.CostEstimate(flops=6 * 128 * tile**3, bytes_accessed=20 * 1024 * 1024, transcendentals=0),
        name="selected_inverse",
    )(
        inverse_block.reshape(rows_local, tile, tile),
        panels.reshape(panels.shape[0], per_group, tile, tile),
        pattern.T,
        active,
    )


def solution(mesh):
    in_specs = (P("row", "col"), P("col", "row", None), P(), P())
    out_specs = P("row", "col")
    return jax.shard_map(
        on_device, mesh=mesh, in_specs=in_specs, out_specs=out_specs, check_vma=False
    )
```

time: 151 us -> 136 us (0.901)
  Pallas kernels: 145 us -> 134 us
  local copies, waits for them, and re-layouts: 4.47 us -> 2.02 us
    pallas_call x1, Pallas kernels: 145 us -> 134 us  [on_device(): pl.pallas_call(kernel, out_shape=pltpu.VMEM((AXIS * AXIS * tile, tile), j...]
    unnamed x1, local copies, waits for them, and re-layouts: 4.47 us -> 2.02 us
where the time goes in v3:
time: 136 us
  Pallas kernels  134 us (99%)
  local copies, waits for them, and re-layouts  2.02 us (1%)
    pallas_call x1, Pallas kernels, on_device(): pl.pallas_call(kernel, out_shape=pltpu.VMEM((AXIS * AXIS * tile, tile), j...  134 us

profile of v3, /device:TPU:1, one launch (start us, length us, event | category | flops | bytes accessed | tf_op | source)
XLA Modules:
  0.0 135.9 jit_solution(67573116001950084)
XLA Ops:
  0.0 133.9 %selected_inverse.1 = f32[4096,256]{1,0:T(8,128)S(1)} custom-call(f32[8,256,256]{2,1,0:T(8,128)} %bitcast.3, f32[2,2,256,256]{3,2,1,0:T(8,128)} %bitcast.4, s32[8,64]{1,0:T(8,128)} %bitcast.5, s32[64]{0:T(128)} %active.1), custom_call_target="tpu_custom_call" | custom-call | flops 12884901888 | bytes 20971520 | tf_op jit(solution)/shard_map/selected_inverse/pallas_call | solution.py:393
  133.9 2.0 %copy.6 = f32[4096,256]{1,0:T(8,128)} copy(f32[4096,256]{1,0:T(8,128)S(1)} %selected_inverse.1) | data formatting | bytes 8388608

commit v4 on v3

--- a/solution.py
+++ b/solution.py
@@ -168,28 +168,27 @@
 
         pl.loop(first, last)(body)
 
-    def multiply(x_at, z_at, total, step, side, part):
+    def multiply(x_at, z_at, total, step, part):
         slot = z_at * (AXIS * AXIS) + x_at * AXIS + y
-        column = (y_hi + side) % 2
-        at = (step, side, slice(None), columns(part))
         for group in range(2):
             for entry in range(2):
                 block = lax.rem(pattern[(group * 2 + core) * 2 + entry, slot], rows_local)
                 high, low = split(pan[x_at, z_at, group, entry].T)
-                from_high = inv_high[column * 2 + group, block, :, columns(part)]
-                from_low = inv_low[column * 2 + group, block, :, columns(part)]
-                value = jnp.dot(high, from_high, preferred_element_type=jnp.float32)
-                value += jnp.dot(low, from_high, preferred_element_type=jnp.float32)
-                value += jnp.dot(high, from_low, preferred_element_type=jnp.float32)
-                if group == 0 and entry == 0:
-                    total[at] = value
-                else:
-                    total[at] += value
+                for side in range(2):
+                    column = (y_hi + side) % 2
+                    from_high = inv_high[column * 2 + group, block, :, columns(part)]
+                    from_low = inv_low[column * 2 + group, block, :, columns(part)]
+                    value = jnp.dot(high, from_high, preferred_element_type=jnp.float32)
+                    value += jnp.dot(low, from_high, preferred_element_type=jnp.float32)
+                    value += jnp.dot(high, from_low, preferred_element_type=jnp.float32)
+                    at = (step, side, slice(None), columns(part))
+                    if group == 0 and entry == 0:
+                        total[at] = value
+                    else:
+                        total[at] += value
 
     def places(step):
-        quarter = step // 2
-        x_at = turn(x, quarter + quarter // 2 * (5 - 2 * quarter))
-        return x_at, (y_lo + 1 + step % 2) % 2
+        return turn(x, (0, 1, -1, 2)[step // 2]), (y_lo + 1 + step % 2) % 2
 
     def cell(ref, step, side, part):
         if part is None:
@@ -219,47 +218,36 @@
             cell(mine, step, side, part), out_rows(x_at, y, part), out_local.at[x_at, part or 0]
         )
 
-    def finish(step, side, part):
+    def stays(step, side):
+        return step % 2 == 1 and side == 0
+
+    def sending(step, side, part):
+        x_at, owner_lo = places(step)
+        if stays(step, side):
+            return keep(step, side, part, x_at)
+        return deliver(step, side, part, x_at, (y_hi + side) % 2 * 2 + owner_lo)
+
+    def finish(step, part):
         x_at, owner_lo = places(step)
         slot = (owner_lo * 2 + core) * (AXIS * AXIS) + x_at * AXIS + y
         factor = -active[slot].astype(jnp.float32)
-        across(step, side, part).wait_recv()
-        at = (step, side, slice(None), columns(part))
-        mine[at] = (mine[at] + take[at]) * factor
-        to_y = (y_hi + side) % 2 * 2 + owner_lo
-
-        @pl.when(to_y == y)
-        def _():
-            keep(step, side, part, x_at).start()
-
-        @pl.when(to_y != y)
-        def _():
-            deliver(step, side, part, x_at, to_y).start()
+        for side in (1, 0):
+            across(step, side, part).wait_recv()
+            at = (step, side, slice(None), columns(part))
+            mine[at] = (mine[at] + take[at]) * factor
+            sending(step, side, part).start()
 
     done = []
 
-    def units(first, count, side, part=None):
-        before = done[-1] if done else None
-
-        def body(i):
-            step = first + i
-            x_at, owner_lo = places(step)
-            multiply(x_at, owner_lo * 2 + 1 - core, give, step, side, part)
+    def unit(step, part=None):
+        x_at, owner_lo = places(step)
+        multiply(x_at, owner_lo * 2 + 1 - core, give, step, part)
+        for side in (1, 0):
             across(step, side, part).start()
-            if before is not None:
-
-                @pl.when(i == 0)
-                def _():
-                    finish(*before)
-
-            @pl.when(i > 0)
-            def _():
-                finish(step - 1, side, part)
-
-            multiply(x_at, owner_lo * 2 + core, mine, step, side, part)
-
-        pl.loop(0, count)(body)
-        done.append((first + count - 1, side, part))
+        if done:
+            finish(*done[-1])
+        multiply(x_at, owner_lo * 2 + core, mine, step, part)
+        done.append((step, part))
 
     def relays(ways, *places_along):
         for by in places_along:
@@ -325,8 +313,8 @@
     relays(near, 2)
     relays(pair, 1)
     arrivals(both, 0)
-    units(0, 2, 1, 0)
-    units(0, 2, 0, 0)
+    unit(0, 0)
+    unit(1, 0)
     relays(pair, -1)
     pair_1[1].wait_recv()
     outer_1[1].wait_recv()
@@ -336,41 +324,28 @@
     far_0[1].wait_recv()
     far_1[1].wait_recv()
     split_inverse(1, y_far)
-    units(0, 2, 1, 1)
-    units(0, 2, 0, 1)
+    unit(0, 1)
+    unit(1, 1)
     arrivals(near, 1, -1, 2)
     arrivals(pair, 1)
-    units(2, 2, 1)
-    units(2, 2, 0)
+    unit(2)
+    unit(3)
     arrivals(pair, -1)
-    units(4, 2, 1)
-    units(4, 2, 0)
+    unit(4)
+    unit(5)
     arrivals(pair, 2)
-    units(6, 2, 1)
-    units(6, 2, 0)
+    unit(6)
+    unit(7)
     finish(*done[-1])
 
-    steps = give.shape[0]
-
-    def settle(number, parts):
-        step, side = number // 2, number % 2
-        x_at, owner_lo = places(step)
-        to_y = (y_hi + side) % 2 * 2 + owner_lo
-        for part in parts:
+    for step, part in done:
+        for side in (1, 0):
             across(step, side, part).wait_send()
-
-        @pl.when(to_y == y)
-        def _():
-            for part in parts:
-                keep(step, side, part, x_at).wait()
-
-        @pl.when(to_y != y)
-        def _():
-            for part in parts:
-                deliver(step, side, part, x_at, to_y).wait_send()
-
-    pl.loop(0, 4)(functools.partial(settle, parts=(0, 1)))
-    pl.loop(4, steps * 2)(functools.partial(settle, parts=(None,)))
+            copy = sending(step, side, part)
+            if stays(step, side):
+                copy.wait()
+            else:
+                copy.wait_send()
     for _, copy in sent:
         copy.wait_send()
     for y_at in (y_pair, y_outer, y_far):

time: 136 us -> 135 us (level)
  Pallas kernels: 134 us -> 132 us
    pallas_call x1, Pallas kernels: 134 us -> 132 us  [on_device(): pl.pallas_call(kernel, out_shape=pltpu.VMEM((AXIS * AXIS * tile, tile), j...]
where the time goes in v4:
time: 135 us; the launch traced here: 134 us
  Pallas kernels  132 us (98%)
  local copies, waits for them, and re-layouts  2.02 us (1%)
    pallas_call x1, Pallas kernels, on_device(): pl.pallas_call(kernel, out_shape=pltpu.VMEM((AXIS * AXIS * tile, tile), j...  132 us

profile of v4, /device:TPU:1, one launch (start us, length us, event | category | flops | bytes accessed | tf_op | source)
XLA Modules:
  0.0 134.3 jit_solution(17141376636764004050)
XLA Ops:
  0.0 132.3 %selected_inverse.1 = f32[4096,256]{1,0:T(8,128)S(1)} custom-call(f32[8,256,256]{2,1,0:T(8,128)} %bitcast.3, f32[2,2,256,256]{3,2,1,0:T(8,128)} %bitcast.4, s32[8,64]{1,0:T(8,128)} %bitcast.5, s32[64]{0:T(128)} %active.1), custom_call_target="tpu_custom_call" | custom-call | flops 12884901888 | bytes 20971520 | tf_op jit(solution)/shard_map/selected_inverse/pallas_call | solution.py:368
  132.3 2.0 %copy.6 = f32[4096,256]{1,0:T(8,128)} copy(f32[4096,256]{1,0:T(8,128)S(1)} %selected_inverse.1) | data formatting | bytes 8388608

commit v5 on v4

--- a/solution.py
+++ b/solution.py
@@ -19,8 +19,8 @@
 
 def kernel(
     inverse_in, panels_in, pattern, active, out,
-    inverse, inv_high, inv_low, pan, give, take, mine,
-    own_sem, inv_send, inv_recv, pan_send, pan_recv, core_send, core_recv, out_send, out_recv, out_local,
+    inverse, inv_high, inv_low, pan, far_pan, give, take, mine, far_give, far_take, far_mine,
+    own_sem, inv_send, inv_recv, pan_send, pan_recv, core_send, core_recv, far_send, far_recv, out_send, out_recv,
 ):
     tile = panels_in.shape[3]
     rows_local = inverse_in.shape[0]
@@ -68,13 +68,13 @@
         return copy
 
     class Way:
-        def __init__(self, group, entry, first, second):
-            self.group, self.entry, self.first, self.second = group, entry, first, second
+        def __init__(self, hold, first, second):
+            self.hold, self.first, self.second = hold, first, second
             self.flying = {}
 
         def view(self, by_first, by_second, half=None):
             by_x, by_z = (by_first, by_second) if self.first == "x" else (by_second, by_first)
-            tile_at = pan.at[turn(x, by_x), turn(z, by_z), self.group, self.entry]
+            tile_at = self.hold(turn(x, by_x), turn(z, by_z))
             return tile_at if half is None else tile_at.at[pl.ds(half * (tile // 2), tile // 2)]
 
         def spread(self, key, axis, at, source=None):
@@ -114,9 +114,9 @@
             self.settle(by)
 
     other = 1 - y_lo
-    near = [Way(y_lo, 0, "x", "z"), Way(y_lo, 1, "z", "x")]
-    pair = [Way(other, 0, "x", "z"), Way(other, 1, "z", "x")]
-    both = near + pair
+    near = [Way(lambda *at: pan.at[*at, y_lo, 0], "x", "z"), Way(lambda *at: pan.at[*at, y_lo, 1], "z", "x")]
+    pair = [Way(lambda *at: pan.at[*at, other, 0], "x", "z"), Way(lambda *at: pan.at[*at, other, 1], "z", "x")]
+    far = [Way(lambda *at: far_pan.at[*at, 0], "x", "z"), Way(lambda *at: far_pan.at[*at, 1], "z", "x")]
 
     swap = push("pan", panels_in.at[other], pan.at[x, z, y_lo], to_pair)
 
@@ -168,32 +168,44 @@
 
         pl.loop(first, last)(body)
 
+    def product(piece, group, entry, slot, outputs):
+        block = lax.rem(pattern[(group * 2 + core) * 2 + entry, slot], rows_local)
+        high, low = split(piece.T)
+        for column, rows, part, total, at in outputs:
+            at_inverse = (column * 2 + group, block, slice(None), columns(part))
+            from_high, from_low = inv_high[at_inverse], inv_low[at_inverse]
+            value = jnp.dot(high[:rows], from_high, preferred_element_type=jnp.float32)
+            value += jnp.dot(low[:rows], from_high, preferred_element_type=jnp.float32)
+            value += jnp.dot(high[:rows], from_low, preferred_element_type=jnp.float32)
+            if group == 0 and entry == 0:
+                total[at] = value
+            else:
+                total[at] += value
+
     def multiply(x_at, z_at, total, step, part):
         slot = z_at * (AXIS * AXIS) + x_at * AXIS + y
         for group in range(2):
             for entry in range(2):
-                block = lax.rem(pattern[(group * 2 + core) * 2 + entry, slot], rows_local)
-                high, low = split(pan[x_at, z_at, group, entry].T)
-                for side in range(2):
-                    column = (y_hi + side) % 2
-                    from_high = inv_high[column * 2 + group, block, :, columns(part)]
-                    from_low = inv_low[column * 2 + group, block, :, columns(part)]
-                    value = jnp.dot(high, from_high, preferred_element_type=jnp.float32)
-                    value += jnp.dot(low, from_high, preferred_element_type=jnp.float32)
-                    value += jnp.dot(high, from_low, preferred_element_type=jnp.float32)
-                    at = (step, side, slice(None), columns(part))
-                    if group == 0 and entry == 0:
-                        total[at] = value
-                    else:
-                        total[at] += value
+                outputs = [
+                    ((y_hi + side) % 2, height(step, side), part, total, place(step, side, part)) for side in range(2)
+                ]
+                product(pan[x_at, z_at, group, entry], group, entry, slot, outputs)
 
     def places(step):
         return turn(x, (0, 1, -1, 2)[step // 2]), (y_lo + 1 + step % 2) % 2
 
+    def stays(step, side):
+        return step % 2 == 1 and side == 0
+
+    def height(step, side):
+        return tile // 2 if step % 2 == 1 and side == 1 else tile
+
+    def place(step, side, part):
+        return step, side, slice(0, height(step, side)), columns(part)
+
     def cell(ref, step, side, part):
-        if part is None:
-            return ref.at[step, side]
-        return ref.at[step, side, :, pl.ds(part * lanes, lanes)]
+        first, width = (0, tile) if part is None else (part * lanes, lanes)
+        return ref.at[step, side, pl.ds(0, height(step, side)), pl.ds(first, width)]
 
     def across(step, side, part):
         return pltpu.make_async_remote_copy(
@@ -202,40 +214,36 @@
             device_id=sibling, device_id_type=MESH,
         )
 
-    def out_rows(x_at, y_at, part):
-        rows = out.at[pl.ds(pl.multiple_of((x_at * AXIS + y_at) * tile, tile), tile)]
-        return rows if part is None else rows.at[:, pl.ds(part * lanes, lanes)]
-
-    def deliver(step, side, part, x_at, to_y):
+    def first_row(x_at, y_at):
+        return pl.multiple_of((x_at * AXIS + y_at) * tile, tile)
+
+    def out_cell(x_at, y_at, rows, part):
+        first, width = (0, tile) if part is None else (part * lanes, lanes)
+        return out.at[pl.ds(first_row(x_at, y_at), rows), pl.ds(first, width)]
+
+    def deliver(step, side, part):
+        x_at, owner_lo = places(step)
         return pltpu.make_async_remote_copy(
-            src_ref=cell(mine, step, side, part), dst_ref=out_rows(x_at, y, part),
+            src_ref=cell(mine, step, side, part), dst_ref=out_cell(x_at, y, height(step, side), part),
             send_sem=out_send.at[step, side, part or 0], recv_sem=out_recv.at[y, x_at, part or 0],
-            device_id=device(x, to_y, z, core), device_id_type=MESH,
+            device_id=device(x, (y_hi + side) % 2 * 2 + owner_lo, z, core), device_id_type=MESH,
         )
 
-    def keep(step, side, part, x_at):
-        return pltpu.make_async_copy(
-            cell(mine, step, side, part), out_rows(x_at, y, part), out_local.at[x_at, part or 0]
-        )
-
-    def stays(step, side):
-        return step % 2 == 1 and side == 0
-
-    def sending(step, side, part):
-        x_at, owner_lo = places(step)
-        if stays(step, side):
-            return keep(step, side, part, x_at)
-        return deliver(step, side, part, x_at, (y_hi + side) % 2 * 2 + owner_lo)
+    def factor_of(slot):
+        return -active[slot].astype(jnp.float32)
 
     def finish(step, part):
         x_at, owner_lo = places(step)
-        slot = (owner_lo * 2 + core) * (AXIS * AXIS) + x_at * AXIS + y
-        factor = -active[slot].astype(jnp.float32)
+        factor = factor_of((owner_lo * 2 + core) * (AXIS * AXIS) + x_at * AXIS + y)
         for side in (1, 0):
             across(step, side, part).wait_recv()
-            at = (step, side, slice(None), columns(part))
-            mine[at] = (mine[at] + take[at]) * factor
-            sending(step, side, part).start()
+            at = place(step, side, part)
+            value = (mine[at] + take[at]) * factor
+            if stays(step, side):
+                out[pl.ds(first_row(x_at, y), tile), columns(part)] = value
+            else:
+                mine[at] = value
+                deliver(step, side, part).start()
 
     done = []
 
@@ -249,6 +257,33 @@
         multiply(x_at, owner_lo * 2 + core, mine, step, part)
         done.append((step, part))
 
+    def far_multiply(x_at, z_at, total, number):
+        slot = z_at * (AXIS * AXIS) + x_at * AXIS + y_far
+        for group in range(2):
+            for entry in range(2):
+                piece = far_pan[x_at, (1 - group) * 2 + z_at % 2, entry]
+                product(piece, group, entry, slot, [(y_hi, tile // 2, None, total, number)])
+
+    def far_across(number):
+        return pltpu.make_async_remote_copy(
+            src_ref=far_give.at[number], dst_ref=far_take.at[number],
+            send_sem=far_send.at[number], recv_sem=far_recv.at[number],
+            device_id=sibling, device_id_type=MESH,
+        )
+
+    def far_unit(number):
+        x_at, _ = places(2 * number)
+        far_multiply(x_at, y_lo * 2 + 1 - core, far_give, number)
+        far_across(number).start()
+        far_multiply(x_at, y_lo * 2 + core, far_mine, number)
+
+    def far_finish(number):
+        x_at, _ = places(2 * number)
+        factor = factor_of((y_lo * 2 + core) * (AXIS * AXIS) + x_at * AXIS + y_far)
+        far_across(number).wait_recv()
+        rows = pl.ds(first_row(x_at, y_far) + tile // 2, tile // 2)
+        out[rows, :] = (far_mine[number] + far_take[number]) * factor
+
     def relays(ways, *places_along):
         for by in places_along:
             for way in ways:
@@ -264,11 +299,17 @@
             for way in ways:
                 way.arrived(by)
 
+    def pass_on(ways):
+        for way in ways:
+            way.pass_on()
+
+    def passed(ways):
+        for way in ways:
+            way.passed()
+
     split_inverse(0, y)
     split_inverse(1, y)
-    for way in near:
-        way.pass_on()
-    turns(near, -1)
+    pass_on(near)
     outer_0[0].wait_recv()
     far_1[0] = relay_inverse(0, 1, y_outer, to_pair)
     outer_0[1] = give_own(1, 1, to_outer)
@@ -277,19 +318,21 @@
         way.start()
     relays(near, 0)
     turns(pair, 0)
-    turns(near, 1)
-    for way in near:
-        way.passed()
+    turns(near, -1, 1)
+    passed(near)
     turns(near, 2)
     pair_0[0].wait_recv()
     far_0[0] = relay_inverse(0, 0, y_pair, to_outer)
+    arrivals(near[:1], 0)
+    crossing = push(
+        "pan", pan.at[x, y_lo * 2 + z % 2, 1 - z // 2, :, :, pl.ds(tile // 2, tile // 2)], far_pan.at[x, z], to_far
+    )
     pair_0[1] = give_own(1, 0, to_pair)
     pair_1[1] = give_own(1, 1, to_pair)
     outer_1[1] = give_own(1, 0, to_outer)
     split_inverse(0, y_pair, 0, cut)
     split_inverse(0, y_outer, cut, rows_local)
-    for way in pair:
-        way.pass_on()
+    pass_on(pair)
     relays(pair, 0)
     relays(near, -1)
     turns(pair, 1, -1)
@@ -299,20 +342,23 @@
     split_inverse(0, y_outer, 0, cut)
     outer_0[1].wait_recv()
     far_1[1] = relay_inverse(1, 1, y_outer, to_pair)
-    for way in pair:
-        way.passed()
+    passed(pair)
     turns(pair, 2)
     relays(near, 1)
     far_1[0].wait_recv()
     far_0[0].wait_recv()
     split_inverse(0, y_far)
+    crossing.wait_recv()
+    for way in far:
+        way.start()
+    turns(far, 0)
+    arrivals(near[1:] + pair, 0)
     pair_0[1].wait_recv()
     far_0[1] = relay_inverse(1, 0, y_pair, to_outer)
     split_inverse(1, y_pair, 0, cut)
     split_inverse(1, y_outer, cut, rows_local)
     relays(near, 2)
     relays(pair, 1)
-    arrivals(both, 0)
     unit(0, 0)
     unit(1, 0)
     relays(pair, -1)
@@ -321,6 +367,9 @@
     split_inverse(1, y_pair, cut, rows_local)
     split_inverse(1, y_outer, 0, cut)
     relays(pair, 2)
+    pass_on(far)
+    turns(far, -1, 1)
+    relays(far, 0)
     far_0[1].wait_recv()
     far_1[1].wait_recv()
     split_inverse(1, y_far)
@@ -333,27 +382,39 @@
     arrivals(pair, -1)
     unit(4)
     unit(5)
+    passed(far)
+    turns(far, 2)
+    relays(far, -1, 1)
     arrivals(pair, 2)
     unit(6)
+    relays(far, 2)
     unit(7)
     finish(*done[-1])
-
+    arrivals(far, 0)
+    far_unit(0)
+    for number, by in enumerate((1, -1, 2), 1):
+        arrivals(far, by)
+        far_unit(number)
+        far_finish(number - 1)
+    far_finish(number)
+    for number in range(AXIS):
+        far_across(number).wait_send()
     for step, part in done:
         for side in (1, 0):
             across(step, side, part).wait_send()
-            copy = sending(step, side, part)
-            if stays(step, side):
-                copy.wait()
-            else:
-                copy.wait_send()
+            if not stays(step, side):
+                deliver(step, side, part).wait_send()
     for _, copy in sent:
         copy.wait_send()
     for y_at in (y_pair, y_outer, y_far):
+        rows = tile // 2 if y_at is y_far else tile
         for by in range(AXIS):
             x_at = turn(x, by)
             for part in (0, 1) if by == 0 else (None,):
+                first, width = (0, tile) if part is None else (part * lanes, lanes)
                 pltpu.make_async_remote_copy(
-                    src_ref=cell(mine, 0, 0, part), dst_ref=out_rows(x_at, y_at, part),
+                    src_ref=mine.at[0, 0, pl.ds(0, rows), pl.ds(first, width)],
+                    dst_ref=out_cell(x_at, y_at, rows, part),
                     send_sem=out_send.at[0, 0, 0], recv_sem=out_recv.at[y_at, x_at, part or 0],
                     device_id=to_pair, device_id_type=MESH,
                 ).wait_recv()
@@ -375,14 +436,19 @@
             pltpu.VMEM((AXIS, rows_local, tile, tile), jnp.bfloat16),
             pltpu.VMEM((AXIS, rows_local, tile, tile), jnp.bfloat16),
             pltpu.VMEM((AXIS, AXIS, 2, per_group, tile, tile), jnp.float32),
+            pltpu.VMEM((AXIS, AXIS, per_group, tile, tile // 2), jnp.float32),
             pltpu.VMEM((steps, 2, tile, tile), jnp.float32),
             pltpu.VMEM((steps, 2, tile, tile), jnp.float32),
             pltpu.VMEM((steps, 2, tile, tile), jnp.float32),
+            pltpu.VMEM((AXIS, tile // 2, tile), jnp.float32),
+            pltpu.VMEM((AXIS, tile // 2, tile), jnp.float32),
+            pltpu.VMEM((AXIS, tile // 2, tile), jnp.float32),
             dma((3,)),
             dma((12,)), dma((12,)),
-            dma((81,)), dma((81,)),
+            dma((122,)), dma((122,)),
             dma((steps, 2, 2)), dma((steps, 2, 2)),
-            dma((steps, 2, 2)), dma((AXIS, AXIS, 2)), dma((AXIS, 2)),
+            dma((AXIS,)), dma((AXIS,)),
+            dma((steps, 2, 2)), dma((AXIS, AXIS, 2)),
         ],
         compiler_params=pltpu.CompilerParams(
             collective_id=0, has_side_effects=True, vmem_limit_bytes=56 * 1024 * 1024

time: 135 us -> 132 us (0.978)
  Pallas kernels: 132 us -> 130 us
    pallas_call x1, Pallas kernels: 132 us -> 130 us  [on_device(): pl.pallas_call(kernel, out_shape=pltpu.VMEM((AXIS * AXIS * tile, tile), j...]
where the time goes in v5:
time: 132 us
  Pallas kernels  130 us (98%)
  local copies, waits for them, and re-layouts  2.02 us (2%)
    pallas_call x1, Pallas kernels, on_device(): pl.pallas_call(kernel, out_shape=pltpu.VMEM((AXIS * AXIS * tile, tile), j...  130 us

profile of v5, /device:TPU:1, one launch (start us, length us, event | category | flops | bytes accessed | tf_op | source)
XLA Modules:
  0.0 132.2 jit_solution(637655459163552849)
XLA Ops:
  0.0 130.2 %selected_inverse.1 = f32[4096,256]{1,0:T(8,128)S(1)} custom-call(f32[8,256,256]{2,1,0:T(8,128)} %bitcast.3, f32[2,2,256,256]{3,2,1,0:T(8,128)} %bitcast.4, s32[8,64]{1,0:T(8,128)} %bitcast.5, s32[64]{0:T(128)} %active.1), custom_call_target="tpu_custom_call" | custom-call | flops 12884901888 | bytes 20971520 | tf_op jit(solution)/shard_map/selected_inverse/pallas_call | solution.py:429
  130.2 2.0 %copy.6 = f32[4096,256]{1,0:T(8,128)} copy(f32[4096,256]{1,0:T(8,128)S(1)} %selected_inverse.1) | data formatting | bytes 8388608

commit v6 on v5

--- a/solution.py
+++ b/solution.py
@@ -67,10 +67,18 @@
         sent.append((kind, copy))
         return copy
 
+    received = []
+
+    def got(*copies):
+        for copy in copies:
+            if not any(copy is known for known in received):
+                copy.wait_recv()
+                received.append(copy)
+
     class Way:
         def __init__(self, hold, first, second):
             self.hold, self.first, self.second = hold, first, second
-            self.flying = {}
+            self.next_to, self.beyond = {}, {}
 
         def view(self, by_first, by_second, half=None):
             by_x, by_z = (by_first, by_second) if self.first == "x" else (by_second, by_first)
@@ -79,46 +87,46 @@
 
         def spread(self, key, axis, at, source=None):
             source = self.view(*at) if source is None else source
-            self.flying[key] = [push("pan", source, self.view(*at), along(axis, by)) for by in (1, -1)]
+            self.next_to[key] = [push("pan", source, self.view(*at), along(axis, by)) for by in (1, -1)]
 
         def relay(self, key, axis, at_below, at_above):
-            up, down = self.flying[key]
-            up.wait_recv()
+            up, down = self.next_to[key]
+            got(up)
             below = self.view(*at_below, half=0)
             far_up = push("pan", below, below, along(axis, 1))
-            down.wait_recv()
+            got(down)
             above = self.view(*at_above, half=1)
-            far_down = push("pan", above, above, along(axis, -1))
-            self.flying[key] = [far_up, far_down]
-
-        def settle(self, key):
-            for copy in self.flying.pop(key):
-                copy.wait_recv()
+            self.beyond[key] = [far_up, push("pan", above, above, along(axis, -1))]
 
         def start(self, source=None):
             self.spread("first", self.first, (0, 0), source)
 
-        def pass_on(self):
+        def on(self):
             self.relay("first", self.first, (-1, 0), (1, 0))
 
-        def passed(self):
-            self.settle("first")
-
         def turn_off(self, by, source=None):
+            if by == 2:
+                got(*self.beyond["first"])
+            elif by != 0:
+                got(*self.next_to["first"])
             self.spread(by, self.second, (by, 0), source)
 
-        def turned_on(self, by):
+        def on_again(self, by):
             self.relay(by, self.second, (by, -1), (by, 1))
-
-        def arrived(self, by):
-            self.settle(by)
 
     other = 1 - y_lo
     near = [Way(lambda *at: pan.at[*at, y_lo, 0], "x", "z"), Way(lambda *at: pan.at[*at, y_lo, 1], "z", "x")]
     pair = [Way(lambda *at: pan.at[*at, other, 0], "x", "z"), Way(lambda *at: pan.at[*at, other, 1], "z", "x")]
     far = [Way(lambda *at: far_pan.at[*at, 0], "x", "z"), Way(lambda *at: far_pan.at[*at, 1], "z", "x")]
 
-    swap = push("pan", panels_in.at[other], pan.at[x, z, y_lo], to_pair)
+    def arrived(ways, by):
+        along_x, along_z = ways
+        got(*along_x.beyond[by])
+        if by == 0:
+            got(*along_z.beyond["first"])
+        else:
+            for at in (0, -1, 1, 2):
+                got(*(along_z.beyond if by == 2 else along_z.next_to)[at])
 
     lanes = tile // 2
     cut = rows_local * 5 // 8
@@ -140,26 +148,11 @@
         return push("inv", held(part, y_at, span), held(part, y_at, span), to)
 
     pair_0, outer_0, pair_1, outer_1, far_0, far_1 = ([None, None] for _ in range(6))
-    pair_0[0] = give_own(0, 0, to_pair)
-    outer_0[0] = give_own(0, 1, to_outer)
-    pair_1[0] = give_own(0, 1, to_pair)
-    outer_1[0] = give_own(0, 0, to_outer)
-
-    for entry, way in enumerate(near):
-        way.start(panels_in.at[y_lo, entry])
-    for entry, way in enumerate(near):
-        way.turn_off(0, panels_in.at[y_lo, entry])
-
     own_copies = [
         pltpu.make_async_copy(inverse_in.at[:, :, pl.ds(part * lanes, lanes)], inverse.at[part, y], own_sem.at[part])
         for part in range(2)
     ]
     own_copies.append(pltpu.make_async_copy(panels_in.at[y_lo], pan.at[x, z, y_lo], own_sem.at[2]))
-    for copy in own_copies:
-        copy.start()
-    for copy in own_copies:
-        copy.wait()
-
     def split_inverse(part, y_at, first=0, last=rows_local):
         def body(block):
             high, low = split(inverse[part, y_at, block])
@@ -167,6 +160,36 @@
             inv_low[y_at, block, :, columns(part)] = low
 
         pl.loop(first, last)(body)
+
+    def split_own():
+        for copy in own_copies:
+            copy.start()
+        for copy in own_copies:
+            copy.wait()
+        split_inverse(0, y)
+        split_inverse(1, y)
+
+    def split_next(part):
+        got(pair_0[part], outer_0[part])
+        split_inverse(part, y_pair, 0, cut)
+        split_inverse(part, y_outer, cut, rows_local)
+
+    def split_rest(part):
+        got(pair_1[part], outer_1[part])
+        split_inverse(part, y_pair, cut, rows_local)
+        split_inverse(part, y_outer, 0, cut)
+
+    def split_far(part):
+        got(far_0[part], far_1[part])
+        split_inverse(part, y_far)
+
+    def to_far_by_pair(part):
+        got(pair_0[part])
+        far_0[part] = relay_inverse(part, 0, y_pair, to_outer)
+
+    def to_far_by_outer(part):
+        got(outer_0[part])
+        far_1[part] = relay_inverse(part, 1, y_outer, to_pair)
 
     def product(piece, group, entry, slot, outputs):
         block = lax.rem(pattern[(group * 2 + core) * 2 + entry, slot], rows_local)
@@ -246,16 +269,24 @@
                 deliver(step, side, part).start()
 
     done = []
+    pending = []
+
+    def flush():
+        while pending:
+            pending.pop()()
 
     def unit(step, part=None):
         x_at, owner_lo = places(step)
+        by = (0, 1, -1, 2)[step // 2]
+        arrived(near, by)
+        arrived(pair, by)
         multiply(x_at, owner_lo * 2 + 1 - core, give, step, part)
         for side in (1, 0):
             across(step, side, part).start()
-        if done:
-            finish(*done[-1])
+        flush()
         multiply(x_at, owner_lo * 2 + core, mine, step, part)
         done.append((step, part))
+        pending.append(functools.partial(finish, step, part))
 
     def far_multiply(x_at, z_at, total, number):
         slot = z_at * (AXIS * AXIS) + x_at * AXIS + y_far
@@ -273,9 +304,12 @@
 
     def far_unit(number):
         x_at, _ = places(2 * number)
+        arrived(far, (0, 1, -1, 2)[number])
         far_multiply(x_at, y_lo * 2 + 1 - core, far_give, number)
         far_across(number).start()
+        flush()
         far_multiply(x_at, y_lo * 2 + core, far_mine, number)
+        pending.append(functools.partial(far_finish, number))
 
     def far_finish(number):
         x_at, _ = places(2 * number)
@@ -284,119 +318,120 @@
         rows = pl.ds(first_row(x_at, y_far) + tile // 2, tile // 2)
         out[rows, :] = (far_mine[number] + far_take[number]) * factor
 
-    def relays(ways, *places_along):
-        for by in places_along:
-            for way in ways:
-                way.turned_on(by)
-
-    def turns(ways, *places_along):
-        for by in places_along:
-            for way in ways:
-                way.turn_off(by)
-
-    def arrivals(ways, *places_along):
-        for by in places_along:
-            for way in ways:
-                way.arrived(by)
-
-    def pass_on(ways):
-        for way in ways:
-            way.pass_on()
-
-    def passed(ways):
-        for way in ways:
-            way.passed()
-
-    split_inverse(0, y)
-    split_inverse(1, y)
-    pass_on(near)
-    outer_0[0].wait_recv()
-    far_1[0] = relay_inverse(0, 1, y_outer, to_pair)
-    outer_0[1] = give_own(1, 1, to_outer)
-    swap.wait_recv()
-    for way in pair:
-        way.start()
-    relays(near, 0)
-    turns(pair, 0)
-    turns(near, -1, 1)
-    passed(near)
-    turns(near, 2)
-    pair_0[0].wait_recv()
-    far_0[0] = relay_inverse(0, 0, y_pair, to_outer)
-    arrivals(near[:1], 0)
+    outer_0[0] = give_own(0, 1, to_outer)
+    swap = push("pan", panels_in.at[other], pan.at[x, z, y_lo], to_pair)
+    outer_1[1] = give_own(1, 0, to_outer)
+    near[1].start(panels_in.at[y_lo, 1])
+    near[0].start(panels_in.at[y_lo, 0])
+    split_own()
+    near[0].turn_off(0, panels_in.at[y_lo, 0])
+    near[1].turn_off(0, panels_in.at[y_lo, 1])
+    near[1].turn_off(-1)
+    near[1].on()
+    near[0].turn_off(-1)
+    pair_0[0] = give_own(0, 0, to_pair)
+    outer_1[0] = give_own(0, 0, to_outer)
+    near[0].on_again(0)
+    got(swap)
+    pair[1].start()
+    pair_1[1] = give_own(1, 1, to_pair)
+    got(swap)
+    pair[0].start()
+    near[1].turn_off(2)
+    near[1].on_again(0)
+    near[0].turn_off(1)
+    pair[0].turn_off(1)
+    got(swap, *near[0].beyond[0], *near[1].beyond["first"])
     crossing = push(
         "pan", pan.at[x, y_lo * 2 + z % 2, 1 - z // 2, :, :, pl.ds(tile // 2, tile // 2)], far_pan.at[x, z], to_far
     )
+    got(swap)
+    pair[1].turn_off(0)
+    pair[1].on()
     pair_0[1] = give_own(1, 0, to_pair)
-    pair_1[1] = give_own(1, 1, to_pair)
-    outer_1[1] = give_own(1, 0, to_outer)
-    split_inverse(0, y_pair, 0, cut)
-    split_inverse(0, y_outer, cut, rows_local)
-    pass_on(pair)
-    relays(pair, 0)
-    relays(near, -1)
-    turns(pair, 1, -1)
-    pair_1[0].wait_recv()
-    outer_1[0].wait_recv()
-    split_inverse(0, y_pair, cut, rows_local)
-    split_inverse(0, y_outer, 0, cut)
-    outer_0[1].wait_recv()
-    far_1[1] = relay_inverse(1, 1, y_outer, to_pair)
-    passed(pair)
-    turns(pair, 2)
-    relays(near, 1)
-    far_1[0].wait_recv()
-    far_0[0].wait_recv()
-    split_inverse(0, y_far)
-    crossing.wait_recv()
-    for way in far:
-        way.start()
-    turns(far, 0)
-    arrivals(near[1:] + pair, 0)
-    pair_0[1].wait_recv()
-    far_0[1] = relay_inverse(1, 0, y_pair, to_outer)
-    split_inverse(1, y_pair, 0, cut)
-    split_inverse(1, y_outer, cut, rows_local)
-    relays(near, 2)
-    relays(pair, 1)
+    got(swap)
+    pair[0].turn_off(0)
+    pair[1].turn_off(-1)
+    pair[1].turn_off(1)
+    to_far_by_pair(0)
+    pair[1].turn_off(2)
+    near[0].on_again(-1)
+    pair_1[0] = give_own(0, 1, to_pair)
+    pair[0].on()
+    split_next(0)
+    near[1].turn_off(1)
+    pair[0].turn_off(-1)
+    outer_0[1] = give_own(1, 1, to_outer)
+    to_far_by_outer(0)
+    got(crossing)
+    far[1].start()
+    pair[0].on_again(0)
+    near[0].on_again(1)
+    split_rest(1)
+    pair[0].turn_off(2)
+    got(crossing)
+    far[0].start()
+    to_far_by_pair(1)
+    near[0].on()
+    pair[1].on_again(0)
+    got(crossing)
+    far[1].turn_off(0)
+    to_far_by_outer(1)
+    pair[0].on_again(-1)
+    pair[0].on_again(1)
+    split_next(1)
+    split_rest(0)
+    pair[1].on_again(2)
+    far[1].on()
+    split_far(0)
+    near[1].on_again(1)
     unit(0, 0)
     unit(1, 0)
-    relays(pair, -1)
-    pair_1[1].wait_recv()
-    outer_1[1].wait_recv()
-    split_inverse(1, y_pair, cut, rows_local)
-    split_inverse(1, y_outer, 0, cut)
-    relays(pair, 2)
-    pass_on(far)
-    turns(far, -1, 1)
-    relays(far, 0)
-    far_0[1].wait_recv()
-    far_1[1].wait_recv()
-    split_inverse(1, y_far)
+    flush()
+    near[0].turn_off(2)
+    far[0].on()
+    pair[1].on_again(-1)
+    split_far(1)
+    near[1].on_again(2)
     unit(0, 1)
+    flush()
+    pair[0].on_again(2)
+    unit(2)
+    flush()
+    near[1].on_again(-1)
+    far[1].turn_off(-1)
+    got(crossing)
+    far[0].turn_off(0)
+    pair[1].on_again(1)
+    far[0].turn_off(-1)
+    unit(3)
     unit(1, 1)
-    arrivals(near, 1, -1, 2)
-    arrivals(pair, 1)
-    unit(2)
-    unit(3)
-    arrivals(pair, -1)
     unit(4)
+    flush()
+    near[0].on_again(2)
     unit(5)
-    passed(far)
-    turns(far, 2)
-    relays(far, -1, 1)
-    arrivals(pair, 2)
+    flush()
+    far[0].turn_off(1)
+    far[1].turn_off(2)
+    far[1].on_again(-1)
+    far[0].turn_off(2)
+    far[1].turn_off(1)
+    far[0].on_again(-1)
     unit(6)
-    relays(far, 2)
+    flush()
+    far[0].on_again(1)
+    far[0].on_again(0)
+    far[1].on_again(2)
+    far[1].on_again(0)
     unit(7)
-    finish(*done[-1])
-    arrivals(far, 0)
+    flush()
+    far[1].on_again(1)
+    far[0].on_again(2)
+    far_unit(2)
+    far_unit(1)
     far_unit(0)
-    for number, by in enumerate((1, -1, 2), 1):
-        arrivals(far, by)
-        far_unit(number)
-        far_finish(number - 1)
-    far_finish(number)
+    far_unit(3)
+    flush()
     for number in range(AXIS):
         far_across(number).wait_send()
     for step, part in done:
@@ -405,6 +440,7 @@
             if not stays(step, side):
                 deliver(step, side, part).wait_send()
     for _, copy in sent:
+        got(copy)
         copy.wait_send()
     for y_at in (y_pair, y_outer, y_far):
         rows = tile // 2 if y_at is y_far else tile

time: 132 us -> 130 us (0.985)
  Pallas kernels: 130 us -> 128 us
    pallas_call x1, Pallas kernels: 130 us -> 128 us  [on_device(): pl.pallas_call(kernel, out_shape=pltpu.VMEM((AXIS * AXIS * tile, tile), j...]
where the time goes in v6:
time: 130 us
  Pallas kernels  128 us (98%)
  local copies, waits for them, and re-layouts  2.02 us (2%)
    pallas_call x1, Pallas kernels, on_device(): pl.pallas_call(kernel, out_shape=pltpu.VMEM((AXIS * AXIS * tile, tile), j...  128 us

profile of v6, /device:TPU:1, one launch (start us, length us, event | category | flops | bytes accessed | tf_op | source)
XLA Modules:
  0.0 129.5 jit_solution(11434622054592504301)
XLA Ops:
  0.0 127.5 %selected_inverse.1 = f32[4096,256]{1,0:T(8,128)S(1)} custom-call(f32[8,256,256]{2,1,0:T(8,128)} %bitcast.3, f32[2,2,256,256]{3,2,1,0:T(8,128)} %bitcast.4, s32[8,64]{1,0:T(8,128)} %bitcast.5, s32[64]{0:T(128)} %active.1), custom_call_target="tpu_custom_call" | custom-call | flops 12884901888 | bytes 20971520 | tf_op jit(solution)/shard_map/selected_inverse/pallas_call | solution.py:465
  127.5 2.0 %copy.6 = f32[4096,256]{1,0:T(8,128)} copy(f32[4096,256]{1,0:T(8,128)S(1)} %selected_inverse.1) | data formatting | bytes 8388608

commit v7 on v6

--- a/solution.py
+++ b/solution.py
@@ -129,17 +129,19 @@
                 got(*(along_z.beyond if by == 2 else along_z.next_to)[at])
 
     lanes = tile // 2
-    cut = rows_local * 5 // 8
-    spans = (pl.ds(0, cut), pl.ds(cut, rows_local - cut))
+    cuts = (rows_local * 4 // 8, rows_local * 6 // 8)
+
+    def span_of(part, span):
+        return (pl.ds(0, cuts[part]), pl.ds(cuts[part], rows_local - cuts[part]))[span]
 
     def columns(part):
         return slice(None) if part is None else slice(part * lanes, (part + 1) * lanes)
 
     def own(part, span):
-        return inverse_in.at[spans[span], :, pl.ds(part * lanes, lanes)]
+        return inverse_in.at[span_of(part, span), :, pl.ds(part * lanes, lanes)]
 
     def held(part, y_at, span):
-        return inverse.at[part, y_at, spans[span]]
+        return inverse.at[part, y_at, span_of(part, span)]
 
     def give_own(part, span, to):
         return push("inv", own(part, span), held(part, y, span), to)
@@ -171,13 +173,13 @@
 
     def split_next(part):
         got(pair_0[part], outer_0[part])
-        split_inverse(part, y_pair, 0, cut)
-        split_inverse(part, y_outer, cut, rows_local)
+        split_inverse(part, y_pair, 0, cuts[part])
+        split_inverse(part, y_outer, cuts[part], rows_local)
 
     def split_rest(part):
         got(pair_1[part], outer_1[part])
-        split_inverse(part, y_pair, cut, rows_local)
-        split_inverse(part, y_outer, 0, cut)
+        split_inverse(part, y_pair, cuts[part], rows_local)
+        split_inverse(part, y_outer, 0, cuts[part])
 
     def split_far(part):
         got(far_0[part], far_1[part])
@@ -431,6 +433,9 @@
     far_unit(1)
     far_unit(0)
     far_unit(3)
+    for _, copy in sent:
+        got(copy)
+        copy.wait_send()
     flush()
     for number in range(AXIS):
         far_across(number).wait_send()
@@ -439,9 +444,6 @@
             across(step, side, part).wait_send()
             if not stays(step, side):
                 deliver(step, side, part).wait_send()
-    for _, copy in sent:
-        got(copy)
-        copy.wait_send()
     for y_at in (y_pair, y_outer, y_far):
         rows = tile // 2 if y_at is y_far else tile
         for by in range(AXIS):

time: 130 us -> 128 us (0.985)
  Pallas kernels: 128 us -> 126 us
    pallas_call x1, Pallas kernels: 128 us -> 126 us  [on_device(): pl.pallas_call(kernel, out_shape=pltpu.VMEM((AXIS * AXIS * tile, tile), j...]
where the time goes in v7:
time: 128 us
  Pallas kernels  126 us (98%)
  local copies, waits for them, and re-layouts  2.02 us (2%)
    pallas_call x1, Pallas kernels, on_device(): pl.pallas_call(kernel, out_shape=pltpu.VMEM((AXIS * AXIS * tile, tile), j...  126 us

profile of v7, /device:TPU:1, one launch (start us, length us, event | category | flops | bytes accessed | tf_op | source)
XLA Modules:
  0.0 128.2 jit_solution(6083467709880110878)
XLA Ops:
  0.0 126.2 %selected_inverse.1 = f32[4096,256]{1,0:T(8,128)S(1)} custom-call(f32[8,256,256]{2,1,0:T(8,128)} %bitcast.3, f32[2,2,256,256]{3,2,1,0:T(8,128)} %bitcast.4, s32[8,64]{1,0:T(8,128)} %bitcast.5, s32[64]{0:T(128)} %active.1), custom_call_target="tpu_custom_call" | custom-call | flops 12884901888 | bytes 20971520 | tf_op jit(solution)/shard_map/selected_inverse/pallas_call | solution.py:467
  126.2 2.0 %copy.6 = f32[4096,256]{1,0:T(8,128)} copy(f32[4096,256]{1,0:T(8,128)S(1)} %selected_inverse.1) | data formatting | bytes 8388608

commit v8 on v7

--- a/solution.py
+++ b/solution.py
@@ -325,9 +325,9 @@
     outer_1[1] = give_own(1, 0, to_outer)
     near[1].start(panels_in.at[y_lo, 1])
     near[0].start(panels_in.at[y_lo, 0])
-    split_own()
     near[0].turn_off(0, panels_in.at[y_lo, 0])
     near[1].turn_off(0, panels_in.at[y_lo, 1])
+    split_own()
     near[1].turn_off(-1)
     near[1].on()
     near[0].turn_off(-1)

time: 128 us -> 128 us (level)
  no operation moved by 1% of the time
where the time goes in v8:
time: 128 us
  Pallas kernels  126 us (98%)
  local copies, waits for them, and re-layouts  2.02 us (2%)
    pallas_call x1, Pallas kernels, on_device(): pl.pallas_call(kernel, out_shape=pltpu.VMEM((AXIS * AXIS * tile, tile), j...  126 us

profile of v8, /device:TPU:1, one launch (start us, length us, event | category | flops | bytes accessed | tf_op | source)
XLA Modules:
  0.0 128.2 jit_solution(7885806921282419600)
XLA Ops:
  0.0 126.2 %selected_inverse.1 = f32[4096,256]{1,0:T(8,128)S(1)} custom-call(f32[8,256,256]{2,1,0:T(8,128)} %bitcast.3, f32[2,2,256,256]{3,2,1,0:T(8,128)} %bitcast.4, s32[8,64]{1,0:T(8,128)} %bitcast.5, s32[64]{0:T(128)} %active.1), custom_call_target="tpu_custom_call" | custom-call | flops 12884901888 | bytes 20971520 | tf_op jit(solution)/shard_map/selected_inverse/pallas_call | solution.py:467
  126.2 2.0 %copy.6 = f32[4096,256]{1,0:T(8,128)} copy(f32[4096,256]{1,0:T(8,128)S(1)} %selected_inverse.1) | data formatting | bytes 8388608
